TPU v7x, 512 devices: a whole 4x8x8 slice. The times are simulated.
512 devices in a mesh: tm: 16 (over y, core), tile: 32 (over x, z).
Axes of the slice: x: 4, y: 8, z: 8, core: 2. Of those that a mesh axis runs over, the one named last changes fastest.
Arguments:
- latents: bfloat16 [32, 64, 2560], P('tm', 'tile'), may hold values from -16 to 16
- frame_slot: int32 [32], replicated, may hold values from 0 to 31, as said below
- lengths: int32 [4], replicated, may hold values from 1 to 16, 32 in all
- w_in: bfloat16 [16, 27, 192], replicated, may hold values from -0.3125 to 0.3125
- bias_in: float32 [192], replicated, may hold values from -3 to 3
- norm_gain: float32 [192], replicated, may hold values from 0.1 to 1.9
- w_mid: bfloat16 [192, 27, 192], replicated, may hold values from -0.078125 to 0.078125
- bias_mid: float32 [192], replicated, may hold values from -3 to 3
Outputs:
- decoded: bfloat16 [32, 64, 160, 192], P('tm', 'tile')
Inputs may be any that keep to these rules, and one draw needn't show every extreme that they name: `frame_slot`: each time position appears once. The lengths sum to 32.
All inputs are finite; a program needn't handle non-finite values.
Results may differ from a plain program's by a relative error of at most 0.013.
Values may be sent and summed in bfloat16 or wider, within the bound.
No kernel may reach another device: no remote copies, remote signals or barrier semaphores. Data moves between devices by JAX's collectives and lax.ppermute only.
A program may use at most 64 MiB of HBM per device.

v0:
```python
import jax
import jax.numpy as jnp
from jax import lax
from jax.sharding import PartitionSpec as P

GROUPS = 32


def shifted(x, axis, by):
    size = lax.axis_size(axis)
    pairs = [(i, i + by) for i in range(size) if 0 <= i + by < size]
    return lax.ppermute(x, axis, pairs)


def padded(cells, sides, width):
    for axis, dim in sides:
        count = lax.axis_size(axis)
        ends = count - 1
        head = lax.slice_in_dim(cells, 0, width, axis=dim)
        tail = lax.slice_in_dim(cells, cells.shape[dim] - width, cells.shape[dim], axis=dim)
        cells = jnp.concatenate(
            [
                lax.ppermute(tail, axis, [(i, (i + 1) % count) for i in range(ends)]),
                cells,
                lax.ppermute(head, axis, [((i + 1) % count, i) for i in range(ends)]),
            ],
            axis=dim,
        )
    return cells


def usable_taps(lengths, first_frame):
    frame_index = first_frame + jnp.arange(2, dtype=jnp.int32)
    rollout_ends = jnp.cumsum(lengths)
    closed = rollout_ends[None, :] <= frame_index[:, None]
    rollout_begin = jnp.sum(jnp.where(closed, lengths[None, :], 0), axis=1)
    sources = frame_index[:, None] - 2 + jnp.arange(3, dtype=jnp.int32)[None, :]
    return (sources >= rollout_begin[:, None]).astype(jnp.bfloat16)


def convolve(extended, usable, weight, tile_rows, width_cells):
    total = None
    for k in range(3):
        frame_list = []
        for i in range(2):
            plane = extended[i + k] * usable[i, k]
            taps_list = []
            for dy in range(3):
                for dx in range(3):
                    taps_list.append(plane[dy : dy + tile_rows, dx : dx + width_cells])
            frame_list.append(jnp.stack(taps_list, axis=2))
        patches = jnp.stack(frame_list, axis=0)
        patches = patches.reshape(2 * tile_rows * width_cells, 9, patches.shape[-1])
        term = jnp.einsum(
            "ckn,nko->co",
            patches,
            weight[:, 9 * k : 9 * k + 9, :],
            preferred_element_type=jnp.float32,
        )
        total = term if total is None else total + term
    return total


def pad_columns(extended):
    return jnp.pad(extended, ((0, 0), (0, 0), (1, 1), (0, 0)))


def body(latents, frame_slot, lengths, w_in, bias_in, norm_gain, w_mid, bias_mid):
    tile_rows = latents.shape[1]
    latent_channels = w_in.shape[0]
    channels = w_in.shape[2]
    width_cells = latents.shape[2] // latent_channels
    first_frame = 2 * lax.axis_index("tm")
    usable = usable_taps(lengths, first_frame)
    targets = first_frame + jnp.arange(2, dtype=jnp.int32)
    onehot = (frame_slot[None, :] == targets[:, None]).astype(jnp.bfloat16)
    shard_piece = lax.all_gather(latents, "tm", axis=0, tiled=True)
    count_rows = shard_piece.shape[0]
    arrived = jnp.dot(
        onehot, shard_piece.reshape(count_rows, -1), preferred_element_type=jnp.float32
    )
    picked = arrived.astype(jnp.bfloat16).reshape(targets.shape[0], tile_rows, latents.shape[2])
    history = shifted(picked, "tm", 1)
    picked = jnp.concatenate([history, picked], axis=0)
    latent_ext = padded(picked, (("tile", 1),), 1)
    latent_ext = pad_columns(latent_ext.reshape(4, tile_rows + 2, width_cells, latent_channels))
    hidden = (convolve(latent_ext, usable, w_in, tile_rows, width_cells) + bias_in).astype(
        jnp.bfloat16
    )
    per_group = channels // GROUPS
    hidden_f = hidden.astype(jnp.float32).reshape(2, tile_rows * width_cells, GROUPS, per_group)
    sum_values = jnp.sum(hidden_f, axis=(1, 3))
    sum_squares = jnp.sum(hidden_f * hidden_f, axis=(1, 3))
    sum_values, sum_squares = lax.psum((sum_values, sum_squares), "tile")
    entries = tile_rows * lax.axis_size("tile") * width_cells * per_group
    average = sum_values / entries
    variance = sum_squares / entries - average * average
    normed = (hidden_f - average[:, None, :, None]) * lax.rsqrt(variance + 1e-06)[:, None, :, None]
    normed = normed.reshape(2 * tile_rows * width_cells, channels) * norm_gain
    activated = (
        jax.nn.silu(normed).astype(jnp.bfloat16).reshape(2, tile_rows, width_cells, channels)
    )
    history = shifted(activated, "tm", 1)
    extended = jnp.concatenate([history, activated], axis=0)
    extended = padded(extended, (("tile", 1),), 1)
    branch = convolve(pad_columns(extended), usable, w_mid, tile_rows, width_cells)
    decoded = hidden.astype(jnp.float32) + branch + bias_mid
    return decoded.astype(jnp.bfloat16).reshape(2, tile_rows, width_cells, channels)


def solution(mesh):
    return jax.shard_map(
        body,
        mesh=mesh,
        in_specs=(P("tm", "tile", None), P(), P(), P(), P(), P(), P(), P()),
        out_specs=P("tm", "tile", None, None),
        check_vma=False,
    )
```

profile of v0, /device:TPU:1, one launch (start us, length us, event | category | flops | bytes accessed | tf_op | source)
XLA Modules:
  0.0 229.6 jit_solution(12066249104183698081)
XLA Ops:
  0.0 22.0 %all_gather.3 = bf16[32,2,2560]{2,1,0:T(2,128)(2,1)S(1)} all-gather(bf16[2,2,2560]{2,1,0:T(2,128)(2,1)} %param.8), channel_id=1, replica_groups=mesh['tm'=16,'tile'=32] {'tm'}, dimensions={0}, use_global_device_ids=true | all-gather | bytes 348160 | tf_op jit(solution)/shard_map/all_gather | solution.py:77
  22.1 0.9 convolution_convert_fusion
  23.0 3.6 %collective-permute-start = (bf16[2,2,2560]{2,1,0:T(2,128)(2,1)S(1)}, bf16[2,2,2560]{2,1,0:T(2,128)(2,1)S(1)}, u32[]{:S(2)}, u32[]{:S(2)}) collective-permute-start(bf16[2,2,2560]{2,1,0:T(2,128)(2,1)S(1)} %reshape.104), channel_id=1, source_target_pairs={{0,32},{32,64},{64,96},{96,128},{128,160},{160,192},{192,224},{224... | collective-permute-start | bytes 61448 | tf_op jit(solution)/shard_map/ppermute | solution.py:12
  26.6 0.8 reduce-window.8
  27.4 0.8 fusion.28
  28.5 1.3 collective-permute-start.2
  29.8 4.0 %collective-permute-start.1 = (bf16[4,1,2560]{2,1,0:T(2,128)(2,1)S(1)}, bf16[4,1,2560]{2,1,0:T(2,128)(2,1)S(1)}, u32[]{:S(2)}, u32[]{:S(2)}) collective-permute-start(bf16[4,1,2560]{2,1,0:T(2,128)(2,1)S(1)} %get-tuple-element.77), channel_id=1, source_target_pairs={{0,1},{1,2},{2,3},{3,4},{4,5},{5,6},{6,7},{7,8},{8,9},{9,10},{10,1... | collective-permute-start | bytes 61448 | tf_op jit(solution)/shard_map/ppermute | solution.py:23
  33.8 0.7 fusion.33
  34.4 0.4 collective-permute-done.1
  35.0 0.5 reshape.105
  35.4 4.0 %fusion.21 = (bf16[4,162,16]{2,1,0:T(8,128)(2,1)S(1)}, bf16[4,162,16]{2,1,0:T(8,128)(2,1)S(1)}, bf16[4,162,16]{2,1,0:T(8,128)(2,1)S(1)}, bf16[4,162,16]{2,1,0:T(...) fusion(bf16[4,4,160,16]{3,2,1,0:T(8,128)(2,1)S(1)} %reshape.105, bf16[]{:T(256)} %bitcast.2, ...), kind=kLoop, calls=%fused_computation.163 | loop fusion | flops 248832 | bytes 206348 | tf_op jit(solution)/shard_map/mul | solution.py:46
  47.7 0.4 reshape.111
  48.2 0.5 fusion.31
  48.7 118.3 %all-reduce.2 = (f32[2,32]{0,1:T(8,128)S(1)}, f32[2,32]{0,1:T(8,128)S(1)}) all-reduce(f32[2,32]{0,1:T(8,128)S(1)} %get-tuple-element.6, f32[2,32]{0,1:T(8,128)S(1)} %get-tuple-element.5), channel_id=1, replica_groups=mesh['tm'=16,'tile'=32] {'tile'}, use_global_device_ids=true, to_apply=%region_5.6 | all-reduce | flops 128 | bytes 1024 | tf_op jit(solution)/shard_map/psum | solution.py:94
  167.2 0.4 mul.162
  168.7 32.3 %collective-permute-start.3 = (bf16[2,2,160,192]{3,2,1,0:T(8,128)(2,1)S(1)}, bf16[2,2,160,192]{3,2,1,0:T(8,128)(2,1)S(1)}, u32[]{:S(2)}, u32[]{:S(2)}) collective-permute-start(bf16[2,2,160,192]{3,2,1,0:T(8,128)(2,1)S(1)} %bitcast.429), channel_id=1, source_target_pairs={{0,32},{32,64},{64,96},{96,128},{128,160},{160,192},{192,224},{224... | collective-permute-start | bytes 737288 | tf_op jit(solution)/shard_map/ppermute | solution.py:12
  200.9 4.0 %collective-permute-done.3 = bf16[2,2,160,192]{3,2,1,0:T(8,128)(2,1)S(1)} collective-permute-done((bf16[2,2,160,192]{3,2,1,0:T(8,128)(2,1)S(1)}, bf16[2,2,160,192]{3,2,1,0:T(8,128)(2,1)S(1)}, u32[]{:S(2)}, u32[]{:S(2)}) %collective-permute-start.3) | collective-permute-done | bytes 245792 | tf_op jit(solution)/shard_map/ppermute | solution.py:12
  205.1 1.3 collective-permute-start.5
  206.4 4.2 %collective-permute-start.4 = (bf16[4,1,160,192]{3,2,1,0:T(8,128)(2,1)S(1)}, bf16[4,1,160,192]{3,2,1,0:T(8,128)(2,1)S(1)}, u32[]{:S(2)}, u32[]{:S(2)}) collective-permute-start(bf16[4,1,160,192]{3,2,1,0:T(8,128)(2,1)S(1)} %get-tuple-element.15), channel_id=1, source_target_pairs={{0,1},{1,2},{2,3},{3,4},{4,5},{5,6},{6,7},{7,8},{8,9},{9,10},{10,1... | collective-permute-start | bytes 737288 | tf_op jit(solution)/shard_map/ppermute | solution.py:23
  210.6 2.3 %collective-permute-done.5 = bf16[4,1,160,192]{3,2,1,0:T(8,128)(2,1)S(1)} collective-permute-done((bf16[4,1,160,192]{3,2,1,0:T(8,128)(2,1)S(1)}, bf16[4,1,160,192]{3,2,1,0:T(8,128)(2,1)S(1)}, u32[]{:S(2)}, u32[]{:S(2)}) %collective-permute-start.5) | collective-permute-done | bytes 245792 | tf_op jit(solution)/shard_map/ppermute | solution.py:25
  212.9 1.5 collective-permute-done.4
  214.4 0.5 select_maximum_fusion
  214.9 3.8 %fusion.18 = (bf16[4,162,192]{2,1,0:T(8,128)(2,1)S(1)}, bf16[4,162,192]{2,1,0:T(8,128)(2,1)S(1)}, bf16[4,162,192]{2,1,0:T(8,128)(2,1)S(1)}, bf16[4,162,192]{2,1,...) fusion(bf16[4,4,162,192]{3,2,1,0:T(8,128)(2,1)S(1)} %select_maximum_fusion, ...), kind=kLoop, calls=%fused_computation.42 | loop fusion | flops 746496 | bytes 2488332 | tf_op jit(solution)/shard_map/mul | solution.py:46
  219.4 0.6 pad_maximum_fusion.2
  221.0 0.6 pad_maximum_fusion.1
  221.8 1.5 copy-done
  223.3 1.1 convolution_bitcast_fusion
  224.5 1.1 convolution_bitcast_fusion.1
  226.3 0.6 pad_maximum_fusion
  227.2 0.4 copy-done.4
  227.6 1.1 fusion.11
  228.7 0.9 copy.172
  (208 shorter events, 11.9 us)
Async XLA Ops:
  23.0 5.3 %collective-permute-start = (bf16[2,2,2560]{2,1,0:T(2,128)(2,1)S(1)}, bf16[2,2,2560]{2,1,0:T(2,128)(2,1)S(1)}, u32[]{:S(2)}, u32[]{:S(2)}) collective-permute-start(bf16[2,2,2560]{2,1,0:T(2,128)(2,1)S(1)} %reshape.104), channel_id=1, source_target_pairs={{0,32},{32,64},{64,96},{96,128},{128,160},{160,192},{192,224},{224... | collective-permute-start | bytes 61448 | tf_op jit(solution)/shard_map/ppermute | solution.py:12
  28.5 6.0 %collective-permute-start.2 = (bf16[4,1,2560]{2,1,0:T(2,128)(2,1)S(1)}, bf16[4,1,2560]{2,1,0:T(2,128)(2,1)S(1)}, u32[]{:S(2)}, u32[]{:S(2)}) collective-permute-start(bf16[4,1,2560]{2,1,0:T(2,128)(2,1)S(1)} %get-tuple-element.78), channel_id=1, source_target_pairs={{1,0},{2,1},{3,2},{4,3},{5,4},{6,5},{7,6},{8,7},{9,8},{10,9},{11,1... | collective-permute-start | bytes 61448 | tf_op jit(solution)/shard_map/ppermute | solution.py:25
  29.8 5.1 %collective-permute-start.1 = (bf16[4,1,2560]{2,1,0:T(2,128)(2,1)S(1)}, bf16[4,1,2560]{2,1,0:T(2,128)(2,1)S(1)}, u32[]{:S(2)}, u32[]{:S(2)}) collective-permute-start(bf16[4,1,2560]{2,1,0:T(2,128)(2,1)S(1)} %get-tuple-element.77), channel_id=1, source_target_pairs={{0,1},{1,2},{2,3},{3,4},{4,5},{5,6},{6,7},{7,8},{8,9},{9,10},{10,1... | collective-permute-start | bytes 61448 | tf_op jit(solution)/shard_map/ppermute | solution.py:23
  43.0 1.4 copy-start.1
  46.0 1.4 copy-start.2
  167.2 1.0 copy-start.3
  168.7 36.3 %collective-permute-start.3 = (bf16[2,2,160,192]{3,2,1,0:T(8,128)(2,1)S(1)}, bf16[2,2,160,192]{3,2,1,0:T(8,128)(2,1)S(1)}, u32[]{:S(2)}, u32[]{:S(2)}) collective-permute-start(bf16[2,2,160,192]{3,2,1,0:T(8,128)(2,1)S(1)} %bitcast.429), channel_id=1, source_target_pairs={{0,32},{32,64},{64,96},{96,128},{128,160},{160,192},{192,224},{224... | collective-permute-start | bytes 737288 | tf_op jit(solution)/shard_map/ppermute | solution.py:12
  205.1 7.8 %collective-permute-start.5 = (bf16[4,1,160,192]{3,2,1,0:T(8,128)(2,1)S(1)}, bf16[4,1,160,192]{3,2,1,0:T(8,128)(2,1)S(1)}, u32[]{:S(2)}, u32[]{:S(2)}) collective-permute-start(bf16[4,1,160,192]{3,2,1,0:T(8,128)(2,1)S(1)} %get-tuple-element.16), channel_id=1, source_target_pairs={{1,0},{2,1},{3,2},{4,3},{5,4},{6,5},{7,6},{8,7},{9,8},{10,9},{11,1... | collective-permute-start | bytes 737288 | tf_op jit(solution)/shard_map/ppermute | solution.py:25
  206.4 8.0 %collective-permute-start.4 = (bf16[4,1,160,192]{3,2,1,0:T(8,128)(2,1)S(1)}, bf16[4,1,160,192]{3,2,1,0:T(8,128)(2,1)S(1)}, u32[]{:S(2)}, u32[]{:S(2)}) collective-permute-start(bf16[4,1,160,192]{3,2,1,0:T(8,128)(2,1)S(1)} %get-tuple-element.15), channel_id=1, source_target_pairs={{0,1},{1,2},{2,3},{3,4},{4,5},{5,6},{6,7},{7,8},{8,9},{9,10},{10,1... | collective-permute-start | bytes 737288 | tf_op jit(solution)/shard_map/ppermute | solution.py:23
  221.6 1.8 copy-start
  226.9 0.7 copy-start.4
where the time goes:
time: 234 us; the launch traced here: 230 us
  blocking collectives  140 us (60%)
  starting transfers between devices  46.6 us (20%)
  local copies, waits for them, and re-layouts  15.1 us (6%)
  other arithmetic  13 us (6%)
  waiting for transfers between devices  8.23 us (4%)
  matrix products  5.09 us (2%)
    psum x1, blocking collectives, body(): sum_values, sum_squares = lax.psum((sum_values, sum_squares), 'tile')  118 us
    ppermute x2, starting transfers between devices, shifted(): return lax.ppermute(x, axis, pairs)  35.8 us
    all_gather x1, blocking collectives, body(): shard_piece = lax.all_gather(latents, 'tm', axis=0, tiled=True)  22 us
    ppermute x2, starting transfers between devices, padded(): lax.ppermute(tail, axis, [(i, (i + 1) % count) for i in range(ends)])  8.18 us
    mul x2, other arithmetic, convolve(): plane = extended[i + k] * usable[i, k]  7.86 us
    another operation x72, local copies, waits for them, and re-layouts, convolve(): frame_list.append(jnp.stack(taps_list, axis=2))  5.39 us
  transfers between devices with their start and end apart: 6, of which 4 were waited for; matrix products, arithmetic and copies ran while one was open for 1% of the time, Pallas kernels for 0%

commit v1 on v0

v1 whole, which is shorter than its diff:
```python
import jax
import jax.numpy as jnp
from jax import lax
from jax.sharding import PartitionSpec as P

GROUPS = 32


def begins(lengths, frame_index):
    ends = jnp.cumsum(lengths)
    closed = ends[None, :] <= frame_index[:, None]
    return jnp.sum(jnp.where(closed, lengths[None, :], 0), axis=1)


def convolve(extended, usable, weight, frames, rows, width):
    total = None
    padded = jnp.pad(extended, ((0, 0), (0, 0), (1, 1), (0, 0)))
    for k in range(3):
        planes = jnp.stack([padded[i + k] * usable[i, k] for i in range(frames)], axis=0)
        taps = []
        for dy in range(3):
            for dx in range(3):
                taps.append(planes[:, dy : dy + rows, dx : dx + width])
        patches = jnp.stack(taps, axis=3).reshape(frames * rows * width, 9, -1)
        term = jnp.einsum(
            "ckn,nko->co",
            patches,
            weight[:, 9 * k : 9 * k + 9, :],
            preferred_element_type=jnp.float32,
        )
        total = term if total is None else total + term
    return total


def body(latents, frame_slot, lengths, w_in, bias_in, norm_gain, w_mid, bias_mid):
    rows = latents.shape[1]
    zc = w_in.shape[0]
    channels = w_in.shape[2]
    width = latents.shape[2] // zc
    per_group = channels // GROUPS
    tiles = lax.axis_size("tile")
    tile = lax.axis_index("tile")
    first = 2 * lax.axis_index("tm")
    own = first + jnp.arange(-4, 2, dtype=jnp.int32)
    onehot = (frame_slot[None, :] == own[:, None]).astype(jnp.bfloat16)
    gathered = lax.all_gather(latents, "tm", axis=0, tiled=True)
    picked = jnp.dot(
        onehot, gathered.reshape(gathered.shape[0], -1), preferred_element_type=jnp.float32
    )
    picked = picked.astype(jnp.bfloat16).reshape(6, rows, -1)
    above = lax.ppermute(picked, "tile", [(i, i + 1) for i in range(tiles - 1)])
    below = lax.ppermute(picked, "tile", [(i + 1, i) for i in range(tiles - 1)])
    ext = jnp.concatenate([above, picked, below], axis=1).reshape(6, 3 * rows, width, zc)

    frames = first + jnp.arange(-2, 2, dtype=jnp.int32)
    begin = begins(lengths, frames)
    sources = frames[:, None] - 2 + jnp.arange(3, dtype=jnp.int32)[None, :]
    usable = (sources >= begin[:, None]).astype(jnp.bfloat16)

    hidden = (convolve(ext, usable, w_in, 4, 4, width) + bias_in).astype(jnp.bfloat16)
    hidden = hidden.reshape(4, 4, width, channels)
    hidden_f = hidden.astype(jnp.float32)
    mine = hidden_f[:, 1:3]
    sums = jnp.stack([jnp.sum(mine, axis=(1, 2)), jnp.sum(mine * mine, axis=(1, 2))], axis=1)
    sums = jnp.sum(sums.reshape(4, 2, GROUPS, per_group), axis=3)
    block = jnp.broadcast_to(sums.reshape(1, 2, 128), (tiles, 2, 128))
    sums = jnp.sum(lax.all_to_all(block, "tile", 0, 0), axis=0).reshape(4, 2, GROUPS)
    entries = rows * tiles * width * per_group
    average = sums[:, 0] / entries
    variance = sums[:, 1] / entries - average * average
    scale = lax.rsqrt(variance + 1e-06)
    average = jnp.repeat(average, per_group, axis=1)[:, None, None, :]
    scale = jnp.repeat(scale, per_group, axis=1)[:, None, None, :]
    activated = jax.nn.silu((hidden_f - average) * scale * norm_gain).astype(jnp.bfloat16)
    grid_rows = rows * tile - 1 + jnp.arange(4)
    inside = (grid_rows >= 0) & (grid_rows < rows * tiles)
    activated = jnp.where(inside[None, :, None, None], activated, jnp.bfloat16(0))
    branch = convolve(activated, usable[2:], w_mid, 2, 2, width)
    decoded = mine[2:].reshape(-1, channels) + branch + bias_mid
    return decoded.astype(jnp.bfloat16).reshape(2, rows, width, channels)


def solution(mesh):
    return jax.shard_map(
        body,
        mesh=mesh,
        in_specs=(P("tm", "tile", None), P(), P(), P(), P(), P(), P(), P()),
        out_specs=P("tm", "tile", None, None),
        check_vma=False,
    )
```

time: 234 us -> 284 us (1.21)
  local copies, waits for them, and re-layouts: 15.1 us -> 187 us
  blocking collectives: 140 us -> 22.1 us
  starting transfers between devices: 46.6 us -> 18.5 us
  other arithmetic: 13 us -> 27.9 us
  matrix products: 5.09 us -> 17.4 us
    psum x1 -> x0, blocking collectives: 118 us -> none  [body(): sum_values, sum_squares = lax.psum((sum_values, sum_squares), 'tile')]
    another operation x78 -> x62, local copies, waits for them, and re-layouts: 6.86 us -> 94.4 us  [the longest x60 94.2 us: convolve(): patches = jnp.stack(taps, axis=3).reshape(frames * rows * width, 9, -1)]
    slice x2 -> x32, local copies, waits for them, and re-layouts: 0.71 us -> 42.4 us  [the longest x30 40.6 us: convolve(): taps.append(planes[:, dy:dy + rows, dx:dx + width])]
    ppermute x6 -> x2, starting transfers between devices: 46.6 us -> 5.28 us  [the longest x1 3.99 us: body(): above = lax.ppermute(picked, 'tile', [(i, i + 1) for i in range(tiles - 1)])]
    unnamed x108 -> x125, local copies, waits for them, and re-layouts: 3.69 us -> 42.1 us
    all_to_all x0 -> x1, starting transfers between devices: none -> 13.2 us  [body(): lax.all_to_all(block, 'tile', 0, 0)]
    dot_general x6, matrix products: 4.22 us -> 16.5 us  [convolve(): jnp.einsum('ckn,nko->co', patches, weight[:, 9 * k:9 * k + 9, :], preferr...]
    ppermute x6 -> x2, waiting for transfers between devices: 8.23 us -> 0.01 us  [the longest x1 0.01 us: body(): below = lax.ppermute(picked, 'tile', [(i + 1, i) for i in range(tiles - 1)])]
  transfers between devices with their start and end apart: 6 -> 3, of which waited for: 4 -> 1; matrix products, arithmetic and copies ran while one was open for 1% -> 2% of each run, Pallas kernels for 0% -> 0%
where the time goes in v1:
time: 284 us; the launch traced here: 280 us
  local copies, waits for them, and re-layouts  187 us (66%)
  other arithmetic  27.9 us (10%)
  blocking collectives  22.1 us (8%)
  starting transfers between devices  18.5 us (7%)
  matrix products  17.4 us (6%)
  waiting for transfers between devices  6.59 us (2%)
    another operation x60, local copies, waits for them, and re-layouts, convolve(): patches = jnp.stack(taps, axis=3).reshape(frames * rows * width, 9, -1)  94.2 us
    unnamed x125, local copies, waits for them, and re-layouts  42.1 us
    slice x30, local copies, waits for them, and re-layouts, convolve(): taps.append(planes[:, dy:dy + rows, dx:dx + width])  40.6 us
    all_gather x1, blocking collectives, body(): gathered = lax.all_gather(latents, 'tm', axis=0, tiled=True)  22.1 us
    dot_general x6, matrix products, convolve(): jnp.einsum('ckn,nko->co', patches, weight[:, 9 * k:9 * k + 9, :], preferr...  16.5 us
    mul x3, other arithmetic, convolve(): padded[i + k] * usable[i, k]  14.3 us
    all_to_all x1, starting transfers between devices, body(): lax.all_to_all(block, 'tile', 0, 0)  13.2 us
    another operation x6, other arithmetic, convolve(): jnp.stack([padded[i + k] * usable[i, k] for i in range(frames)], axis=0)  8.78 us
  transfers between devices with their start and end apart: 3, of which 1 were waited for; matrix products, arithmetic and copies ran while one was open for 2% of the time, Pallas kernels for 0%

profile of v1, /device:TPU:1, one launch (start us, length us, event | category | flops | bytes accessed | tf_op | source)
XLA Modules:
  0.0 280.1 jit_solution(132684978406560665)
XLA Ops:
  0.0 22.1 %all_gather.3 = bf16[32,2,2560]{2,1,0:T(2,128)(2,1)S(1)} all-gather(bf16[2,2,2560]{2,1,0:T(2,128)(2,1)} %param.8), channel_id=1, replica_groups=mesh['tm'=16,'tile'=32] {'tm'}, dimensions={0}, use_global_device_ids=true | all-gather | bytes 348160 | tf_op jit(solution)/shard_map/all_gather | solution.py:46
  24.4 4.0 %collective-permute-start = (bf16[6,2,2560]{2,1,0:T(2,128)(2,1)S(1)}, bf16[6,2,2560]{2,1,0:T(2,128)(2,1)S(1)}, u32[]{:S(2)}, u32[]{:S(2)}) collective-permute-start(bf16[6,2,2560]{2,1,0:T(2,128)(2,1)S(1)} %reshape.202), channel_id=1, source_target_pairs={{0,1},{1,2},{2,3},{3,4},{4,5},{5,6},{6,7},{7,8},{8,9},{9,10},{10,1... | collective-permute-start | bytes 184328 | tf_op jit(solution)/shard_map/ppermute | solution.py:51
  31.6 2.6 slice_multiply_fusion.5
  34.2 6.3 %slice_multiply_fusion.1 = (bf16[1,6,162,16]{2,3,1,0:T(8,128)(2,1)}, bf16[1,6,162,16]{2,3,1,0:T(8,128)(2,1)}, bf16[1,6,162,16]{2,3,1,0:T(8,128)(2,1)S(1)}, bf16[...) fusion(bf16[6,6,162,16]{2,3,1,0:T(8,128)(2,1)S(1)} %fusion.42, ...), kind=kLoop, calls=%fused_computation.176 | loop fusion | flops 139968 | bytes 435474 | tf_op jit(solution)/shard_map/mul | solution.py:19
  108.8 2.7 convolution_bitcast_fusion
  111.7 2.7 convolution_bitcast_fusion.1
  148.9 4.0 %fusion.4 = f32[2560,192]{0,1:T(8,128)} fusion(f32[2560,192]{0,1:T(8,128)} %convolution_bitcast_fusion, f32[2560,192]{0,1:T(8,128)} %convolution_bitcast_fusion.1, bf16[2560,9,16]{0,2,1:T(8,128)(2,1)S(1)} %constant_dynamic-update-slice_fusion, f32[192]{0:T(256)S(1)} %copy-done.35, bf16[16,27,192]{2,0,1:T(8,128)(2,1)} %param.11), kind=kOutput, calls=%fused_computation.8 | convolution fusion | flops 144015360 | bytes 6710016 | tf_op jit(solution)/shard_map/ckn,nko->co/dot_general | solution.py:25
  152.9 3.1 %copy.329 = f32[2560,192]{1,0:T(8,128)} copy(f32[2560,192]{0,1:T(8,128)} %fusion.4) | data formatting | bytes 3932160 | tf_op jit(solution)/shard_map/convert_element_type | solution.py:62
  158.6 13.2 %all-to-all-start = ((f32[32,2,128]{2,1,0:T(2,128)}), f32[32,2,128]{2,1,0:T(2,128)S(1)}, u32[]{:S(2)}, u32[]{:S(2)}) async-start(f32[32,2,128]{2,1,0:T(2,128)} %broadcast_in_dim.53), calls=%async_computation | async-start | bytes 65536 | tf_op jit(solution)/shard_map/all_to_all | solution.py:67
  174.0 6.6 %all-to-all-done = f32[32,2,128]{2,1,0:T(2,128)S(1)} async-done(((f32[32,2,128]{2,1,0:T(2,128)}), f32[32,2,128]{2,1,0:T(2,128)S(1)}, u32[]{:S(2)}, u32[]{:S(2)}) %all-to-all-start) | async-done | bytes 32800 | tf_op jit(solution)/shard_map/all_to_all | solution.py:67
  181.1 2.6 fusion.5
  183.7 5.4 %broadcast_multiply_fusion.3 = (bf16[1,4,162,192]{3,2,1,0:T(8,128)(2,1)S(1)}, bf16[1,4,162,192]{3,2,1,0:T(8,128)(2,1)S(1)}, bf16[1,4,162,192]{3,2,1,0:T(8,128)(2...) fusion(bf16[]{:T(256)} %bitcast.5, ...), kind=kLoop, calls=%fused_computation.116 | loop fusion | flops 2985984 | bytes 2476044 | tf_op jit(solution)/shard_map/mul | solution.py:19
  190.9 1.8 copy.352
  194.4 1.8 copy.353
  198.1 1.8 copy.355
  199.9 1.8 copy.356
  201.7 1.9 copy.357
  203.6 1.9 copy.358
  207.3 1.8 copy.360
  209.1 4.2 %pad_maximum_fusion.1 = (bf16[2,2,160,192]{3,2,1,0:T(8,128)(2,1)}, bf16[2,2,160,192]{3,2,1,0:T(8,128)(2,1)}, bf16[2,2,160,192]{3,2,1,0:T(8,128)(2,1)}, bf16[2,2,...) fusion(bf16[1,4,162,192]{3,2,1,0:T(8,128)(2,1)} %get-tuple-elem, ...), kind=kLoop, calls=%fused_computation.106 | loop fusion | flops 4423680 | bytes 2709504 | tf_op jit(solution)/shard_map/stack | solution.py:19
  220.5 1.8 copy.345
  222.3 1.8 copy.346
  224.2 1.8 copy.347
  227.8 1.8 copy.349
  242.1 3.3 %convolution_bitcast_fusion.3 = f32[640,192]{0,1:T(8,128)} fusion(bf16[192,27,192]{2,0,1:T(8,128)(2,1)S(1)} %copy-done, bf16[640,9,192]{0,2,1:T(8,128)(2,1)} %constant_dynamic-update-slice_fusion.45), kind=kOutput, calls=%fused_computation.61 | convolution fusion | flops 424673280 | bytes 4694016 | tf_op jit(solution)/shard_map/ckn,nko->co/dot_general | solution.py:25
  249.9 1.9 copy.332
  253.5 1.8 copy.333
  255.3 1.8 copy.334
  257.2 1.8 copy.335
  259.0 1.8 copy.336
  262.6 1.8 copy.338
  276.9 2.4 fusion.10
  (241 shorter events, 163.2 us)
Async XLA Ops:
  0.0 242.0 %copy-start = (bf16[192,27,192]{2,0,1:T(8,128)(2,1)S(1)}, bf16[192,27,192]{2,0,1:T(8,128)(2,1)}, u32[]{:S(2)}) copy-start(bf16[192,27,192]{2,0,1:T(8,128)(2,1)} %param.14) | copy-start | bytes 5971972
  0.0 29.1 %copy-start.37 = (s32[4]{0:T(128)S(1)}, s32[4]{0:T(128)}, u32[]{:S(2)}) copy-start(s32[4]{0:T(128)} %param.10) | copy-start | bytes 52
  23.1 7.1 %collective-permute-start.1 = (bf16[6,2,2560]{2,1,0:T(2,128)(2,1)S(1)}, bf16[6,2,2560]{2,1,0:T(2,128)(2,1)S(1)}, u32[]{:S(2)}, u32[]{:S(2)}) collective-permute-start(bf16[6,2,2560]{2,1,0:T(2,128)(2,1)S(1)} %reshape.202), channel_id=1, source_target_pairs={{1,0},{2,1},{3,2},{4,3},{5,4},{6,5},{7,6},{8,7},{9,8},{10,9},{11,1... | collective-permute-start | bytes 184328 | tf_op jit(solution)/shard_map/ppermute | solution.py:52
  24.4 6.4 %collective-permute-start = (bf16[6,2,2560]{2,1,0:T(2,128)(2,1)S(1)}, bf16[6,2,2560]{2,1,0:T(2,128)(2,1)S(1)}, u32[]{:S(2)}, u32[]{:S(2)}) collective-permute-start(bf16[6,2,2560]{2,1,0:T(2,128)(2,1)S(1)} %reshape.202), channel_id=1, source_target_pairs={{0,1},{1,2},{2,3},{3,4},{4,5},{5,6},{6,7},{7,8},{8,9},{9,10},{10,1... | collective-permute-start | bytes 184328 | tf_op jit(solution)/shard_map/ppermute | solution.py:51
  99.6 11.8 %copy-start.21 = (bf16[2560,1,16]{0,2,1:T(8,128)(2,1)S(1)}, bf16[2560,1,16]{0,2,1:T(8,128)(2,1)}, u32[]{:S(2)}) copy-start(bf16[2560,1,16]{0,2,1:T(8,128)(2,1)} %stack.238) | copy-start | bytes 245764
  99.6 11.9 %copy-start.22 = (bf16[2560,1,16]{0,2,1:T(8,128)(2,1)S(1)}, bf16[2560,1,16]{0,2,1:T(8,128)(2,1)}, u32[]{:S(2)}) copy-start(bf16[2560,1,16]{0,2,1:T(8,128)(2,1)} %stack.239) | copy-start | bytes 245764
  101.4 10.1 %copy-start.18 = (bf16[2560,9,16]{0,2,1:T(8,128)(2,1)S(1)}, bf16[2560,9,16]{0,2,1:T(8,128)(2,1)}, u32[]{:S(2)}) copy-start(bf16[2560,9,16]{0,2,1:T(8,128)(2,1)} %constant_dynamic-update-slice_fusion.17) | copy-start | bytes 2211844
  101.4 10.1 %copy-start.23 = (bf16[2560,1,16]{0,2,1:T(8,128)(2,1)S(1)}, bf16[2560,1,16]{0,2,1:T(8,128)(2,1)}, u32[]{:S(2)}) copy-start(bf16[2560,1,16]{0,2,1:T(8,128)(2,1)} %stack.240) | copy-start | bytes 245764
  102.4 9.2 %copy-start.24 = (bf16[2560,1,16]{0,2,1:T(8,128)(2,1)S(1)}, bf16[2560,1,16]{0,2,1:T(8,128)(2,1)}, u32[]{:S(2)}) copy-start(bf16[2560,1,16]{0,2,1:T(8,128)(2,1)} %stack.241) | copy-start | bytes 245764
  103.3 8.3 %copy-start.25 = (bf16[2560,1,16]{0,2,1:T(8,128)(2,1)S(1)}, bf16[2560,1,16]{0,2,1:T(8,128)(2,1)}, u32[]{:S(2)}) copy-start(bf16[2560,1,16]{0,2,1:T(8,128)(2,1)} %stack.242) | copy-start | bytes 245764
  104.2 7.4 %copy-start.26 = (bf16[2560,1,16]{0,2,1:T(8,128)(2,1)S(1)}, bf16[2560,1,16]{0,2,1:T(8,128)(2,1)}, u32[]{:S(2)}) copy-start(bf16[2560,1,16]{0,2,1:T(8,128)(2,1)} %stack.243) | copy-start | bytes 245764
  105.1 6.5 %copy-start.27 = (bf16[2560,1,16]{0,2,1:T(8,128)(2,1)S(1)}, bf16[2560,1,16]{0,2,1:T(8,128)(2,1)}, u32[]{:S(2)}) copy-start(bf16[2560,1,16]{0,2,1:T(8,128)(2,1)} %stack.244) | copy-start | bytes 245764
  106.1 5.6 %copy-start.28 = (bf16[2560,1,16]{0,2,1:T(8,128)(2,1)S(1)}, bf16[2560,1,16]{0,2,1:T(8,128)(2,1)}, u32[]{:S(2)}) copy-start(bf16[2560,1,16]{0,2,1:T(8,128)(2,1)} %stack.245) | copy-start | bytes 245764
  122.4 26.6 %copy-start.35 = (f32[192]{0:T(256)S(1)}, f32[192]{0:T(256)}, u32[]{:S(2)}) copy-start(f32[192]{0:T(256)} %param.12) | copy-start | bytes 2308
  156.0 25.1 %copy-start.34 = (f32[192]{0:T(256)S(1)}, f32[192]{0:T(256)}, u32[]{:S(2)}) copy-start(f32[192]{0:T(256)} %param.13) | copy-start | bytes 2308
  158.6 22.0 %all-to-all-start = ((f32[32,2,128]{2,1,0:T(2,128)}), f32[32,2,128]{2,1,0:T(2,128)S(1)}, u32[]{:S(2)}, u32[]{:S(2)}) async-start(f32[32,2,128]{2,1,0:T(2,128)} %broadcast_in_dim.53), calls=%async_computation | async-start | bytes 65536 | tf_op jit(solution)/shard_map/all_to_all | solution.py:67
  231.5 8.4 %copy-start.6 = (bf16[640,1,192]{0,2,1:T(8,128)(2,1)S(1)}, bf16[640,1,192]{0,2,1:T(8,128)(2,1)}, u32[]{:S(2)}) copy-start(bf16[640,1,192]{0,2,1:T(8,128)(2,1)} %copy.358) | copy-start | bytes 737284
  231.5 9.1 %copy-start.4 = (bf16[640,1,192]{0,2,1:T(8,128)(2,1)S(1)}, bf16[640,1,192]{0,2,1:T(8,128)(2,1)}, u32[]{:S(2)}) copy-start(bf16[640,1,192]{0,2,1:T(8,128)(2,1)} %copy.359) | copy-start | bytes 737284
  231.5 9.8 %copy-start.5 = (bf16[640,1,192]{0,2,1:T(8,128)(2,1)S(1)}, bf16[640,1,192]{0,2,1:T(8,128)(2,1)}, u32[]{:S(2)}) copy-start(bf16[640,1,192]{0,2,1:T(8,128)(2,1)} %copy.360) | copy-start | bytes 737284
  241.3 4.1 %copy-start.13 = (bf16[640,1,192]{0,2,1:T(8,128)(2,1)S(1)}, bf16[640,1,192]{0,2,1:T(8,128)(2,1)}, u32[]{:S(2)}) copy-start(bf16[640,1,192]{0,2,1:T(8,128)(2,1)} %copy.343) | copy-start | bytes 737284
  241.3 4.1 %copy-start.33 = (bf16[640,9,192]{0,2,1:T(8,128)(2,1)S(1)}, bf16[640,9,192]{0,2,1:T(8,128)(2,1)}, u32[]{:S(2)}) copy-start(bf16[640,9,192]{0,2,1:T(8,128)(2,1)} %constant_dynamic-update-slice_fusion.44) | copy-start | bytes 6635524
  242.0 3.5 %copy-start.11 = (bf16[640,1,192]{0,2,1:T(8,128)(2,1)S(1)}, bf16[640,1,192]{0,2,1:T(8,128)(2,1)}, u32[]{:S(2)}) copy-start(bf16[640,1,192]{0,2,1:T(8,128)(2,1)} %copy.346) | copy-start | bytes 737284
  242.0 3.6 %copy-start.10 = (bf16[640,1,192]{0,2,1:T(8,128)(2,1)S(1)}, bf16[640,1,192]{0,2,1:T(8,128)(2,1)}, u32[]{:S(2)}) copy-start(bf16[640,1,192]{0,2,1:T(8,128)(2,1)} %copy.347) | copy-start | bytes 737284
  249.9 14.6 %copy-start.3 = (bf16[2,2,160,192]{3,2,1,0:T(8,128)(2,1)S(1)}, bf16[2,2,160,192]{3,2,1,0:T(8,128)(2,1)}, u32[]{:S(2)}) copy-start(bf16[2,2,160,192]{3,2,1,0:T(8,128)(2,1)} %get-tuple-element.21) | copy-start | bytes 737284
  251.8 13.6 %copy-start.2 = (bf16[2,2,160,192]{3,2,1,0:T(8,128)(2,1)S(1)}, bf16[2,2,160,192]{3,2,1,0:T(8,128)(2,1)}, u32[]{:S(2)}) copy-start(bf16[2,2,160,192]{3,2,1,0:T(8,128)(2,1)} %get-tuple-element.13) | copy-start | bytes 737284
  265.3 11.5 %copy-start.1 = (f32[640,192]{0,1:T(8,128)S(1)}, f32[640,192]{0,1:T(8,128)}, u32[]{:S(2)}) copy-start(f32[640,192]{0,1:T(8,128)} %copy.362) | copy-start | bytes 1474564
  265.4 11.5 %copy-start.36 = (f32[192]{0:T(256)S(1)}, f32[192]{0:T(256)}, u32[]{:S(2)}) copy-start(f32[192]{0:T(256)} %param.15) | copy-start | bytes 2308
  266.2 8.5 %copy-start.17 = (bf16[640,1,192]{0,2,1:T(8,128)(2,1)S(1)}, bf16[640,1,192]{0,2,1:T(8,128)(2,1)}, u32[]{:S(2)}) copy-start(bf16[640,1,192]{0,2,1:T(8,128)(2,1)} %copy.338) | copy-start | bytes 737284
  266.2 9.2 %copy-start.15 = (bf16[640,1,192]{0,2,1:T(8,128)(2,1)S(1)}, bf16[640,1,192]{0,2,1:T(8,128)(2,1)}, u32[]{:S(2)}) copy-start(bf16[640,1,192]{0,2,1:T(8,128)(2,1)} %copy.339) | copy-start | bytes 737284
  266.2 9.9 %copy-start.16 = (bf16[640,1,192]{0,2,1:T(8,128)(2,1)S(1)}, bf16[640,1,192]{0,2,1:T(8,128)(2,1)}, u32[]{:S(2)}) copy-start(bf16[640,1,192]{0,2,1:T(8,128)(2,1)} %copy.340) | copy-start | bytes 737284
  266.2 10.6 %copy-start.19 = (f32[640,192]{0,1:T(8,128)S(1)}, f32[640,192]{0,1:T(8,128)}, u32[]{:S(2)}) copy-start(f32[640,192]{0,1:T(8,128)} %convolution_bitcast_fusion.3) | copy-start | bytes 1474564
  266.2 10.6 %copy-start.20 = (f32[640,192]{0,1:T(8,128)S(1)}, f32[640,192]{0,1:T(8,128)}, u32[]{:S(2)}) copy-start(f32[640,192]{0,1:T(8,128)} %convolution_bitcast_fusion.4) | copy-start | bytes 1474564
  (9 other events, 21.6 us)

commit v2 on v1

v2 whole, which is shorter than its diff:
```python
import jax
import jax.numpy as jnp
from jax import lax
from jax.experimental import pallas as pl
from jax.experimental.pallas import tpu as pltpu
from jax.sharding import PartitionSpec as P

GROUPS = 32
LANES = 256
VMEM = pl.BlockSpec(memory_space=pltpu.VMEM)
SMEM = pl.BlockSpec(memory_space=pltpu.SMEM)
F32 = jnp.float32
BF16 = jnp.bfloat16
PARAMS = pltpu.CompilerParams(vmem_limit_bytes=48 * 1024 * 1024)


def usable(lengths_ref, frame, k):
    begin = jnp.int32(0)
    end = jnp.int32(0)
    for r in range(lengths_ref.shape[0]):
        end = end + lengths_ref[r]
        begin = jnp.where(end <= frame, end, begin)
    return (frame - 2 + k) >= begin


def roll_both(v):
    return pltpu.roll(v, 1, 1), pltpu.roll(v, LANES - 1, 1)


def pick_kernel(slot_ref, gathered_ref, picked_ref):
    base = 2 * lax.axis_index("tm") - 4
    picked_ref[...] = jnp.zeros_like(picked_ref)

    @pl.loop(0, slot_ref.shape[0])
    def _(p):
        j = slot_ref[p] - base

        @pl.when((j >= 0) & (j < 6))
        def _():
            picked_ref[j] = gathered_ref[p]


def group_mask(channels, frame):
    per_group = channels // GROUPS
    channel = lax.broadcasted_iota(jnp.int32, (channels, 128), 0)
    lane = lax.broadcasted_iota(jnp.int32, (channels, 128), 1)
    low = (lane - GROUPS * frame) * per_group
    return (channel >= low) & (channel < low + per_group) & (lane >= GROUPS * frame) & (lane < GROUPS * frame + GROUPS)


def hidden_kernel(width, lengths_ref, above_ref, picked_ref, below_ref, w_ref, bias_ref, hidden_ref, sums_ref, xs_ref):
    channels = bias_ref.shape[0]
    first = 2 * lax.axis_index("tm")
    for f in range(6):
        for r in range(6):
            ref = (above_ref, picked_ref, below_ref)[r // 2]
            v = ref[f, r % 2]
            left, right = roll_both(v.astype(F32))
            xs_ref[f, r, 0:16] = left.astype(BF16)
            xs_ref[f, r, 16:32] = v
            xs_ref[f, r, 32:48] = right.astype(BF16)
    bias = bias_ref[...]
    inside = lax.broadcasted_iota(jnp.int32, (channels, LANES), 1) < width
    columns = []
    for j in range(4):
        frame = first - 2 + j
        u0 = usable(lengths_ref, frame, 0).astype(F32)
        u1 = usable(lengths_ref, frame, 1).astype(F32)
        s1 = jnp.zeros((channels, LANES), F32)
        s2 = jnp.zeros((channels, LANES), F32)
        for r in range(4):
            acc = [
                jnp.dot(w_ref[k], xs_ref[j + k, r : r + 3].reshape(144, LANES), preferred_element_type=F32)
                for k in range(3)
            ]
            h = (acc[2] + u1 * acc[1] + u0 * acc[0] + bias).astype(BF16)
            hidden_ref[j, r] = h
            if r in (1, 2):
                hf = jnp.where(inside, h.astype(F32), 0.0)
                s1 = s1 + hf
                s2 = s2 + hf * hf
        columns.append(
            (
                jnp.sum(s1[:, :128] + s1[:, 128:], axis=1, keepdims=True),
                jnp.sum(s2[:, :128] + s2[:, 128:], axis=1, keepdims=True),
            )
        )
    d1 = jnp.zeros((channels, 128), F32)
    d2 = jnp.zeros((channels, 128), F32)
    for j in range(4):
        mask = group_mask(channels, j)
        d1 = jnp.where(mask, columns[j][0], d1)
        d2 = jnp.where(mask, columns[j][1], d2)
    s1 = jnp.sum(d1, axis=0, keepdims=True)
    s2 = jnp.sum(d2, axis=0, keepdims=True)
    block = jnp.concatenate([s1, s2], axis=0)
    sums_ref[...] = jnp.broadcast_to(block[None], sums_ref.shape)


def decode_kernel(width, entries, tiles, lengths_ref, sums_ref, hidden_ref, w_ref, gain_ref, bias_ref, out_ref, act_ref):
    channels = bias_ref.shape[0]
    first = 2 * lax.axis_index("tm")
    tile = lax.axis_index("tile")
    total = jnp.sum(sums_ref[...], axis=0)
    average = total[0:1] / entries
    variance = total[1:2] / entries - average * average
    rstd = lax.rsqrt(variance + 1e-06)
    lane = lax.broadcasted_iota(jnp.int32, (channels, LANES), 1)
    half_gain = 0.5 * gain_ref[...]
    for j in range(4):
        mask = group_mask(channels, j)
        mean = jnp.sum(jnp.where(mask, average, 0.0), axis=1, keepdims=True)
        scale = jnp.sum(jnp.where(mask, rstd, 0.0), axis=1, keepdims=True) * half_gain
        for r in range(4):
            limit = jnp.int32(width)
            if r == 0:
                limit = jnp.where(tile > 0, limit, 0)
            if r == 3:
                limit = jnp.where(tile < tiles - 1, limit, 0)
            u = (hidden_ref[j, r].astype(F32) - mean) * scale
            a = jnp.where(lane < limit, u + u * jnp.tanh(u), 0.0)
            left, right = roll_both(a)
            act_ref[j, r, 0] = left.astype(BF16)
            act_ref[j, r, 1] = a.astype(BF16)
            act_ref[j, r, 2] = right.astype(BF16)
    bias = bias_ref[...]
    for i in range(2):
        u0 = usable(lengths_ref, first + i, 0)
        u1 = usable(lengths_ref, first + i, 1)
        for r in range(2):
            acc = []
            for k in range(3):
                total = None
                for dy in range(3):
                    for dx in range(3):
                        term = jnp.dot(w_ref[9 * k + 3 * dy + dx], act_ref[i + k, r + dy, dx], preferred_element_type=F32)
                        total = term if total is None else total + term
                acc.append(total)
            y = acc[2] + jnp.where(u1, acc[1], 0.0) + jnp.where(u0, acc[0], 0.0)
            y = y + bias + hidden_ref[2 + i, r + 1].astype(F32)
            out_ref[i, r] = y.T[:width].astype(BF16)


def body(latents, frame_slot, lengths, w_in, bias_in, norm_gain, w_mid, bias_mid):
    rows = latents.shape[1]
    zc = w_in.shape[0]
    channels = w_in.shape[2]
    width = latents.shape[2] // zc
    tiles = lax.axis_size("tile")
    lt = jnp.swapaxes(latents.reshape(2, rows, width, zc), 2, 3)
    lt = jnp.pad(lt, ((0, 0), (0, 0), (0, 0), (0, LANES - width)))
    gathered = lax.all_gather(lt, "tm", axis=0, tiled=True)
    picked = pl.pallas_call(
        pick_kernel,
        out_shape=jax.ShapeDtypeStruct((6, rows, zc, LANES), BF16),
        in_specs=[SMEM, VMEM],
        out_specs=VMEM,
        compiler_params=PARAMS,
        name="pick",
    )(frame_slot, gathered)
    above = lax.ppermute(picked, "tile", [(i, i + 1) for i in range(tiles - 1)])
    below = lax.ppermute(picked, "tile", [(i + 1, i) for i in range(tiles - 1)])
    w_in_t = jnp.transpose(w_in.reshape(zc, 3, 9, channels), (1, 3, 2, 0)).reshape(3, channels, 9 * zc)
    w_mid_t = jnp.transpose(w_mid, (1, 2, 0))

    def hidden_body(*refs):
        hidden_kernel(width, *refs)

    hidden, sums = pl.pallas_call(
        hidden_body,
        out_shape=[
            jax.ShapeDtypeStruct((4, 4, channels, LANES), BF16),
            jax.ShapeDtypeStruct((tiles, 2, 128), F32),
        ],
        in_specs=[SMEM] + [VMEM] * 5,
        out_specs=[VMEM, VMEM],
        scratch_shapes=[pltpu.VMEM((6, 6, 3 * zc, LANES), BF16)],
        compiler_params=PARAMS,
        name="hidden",
    )(lengths, above, picked, below, w_in_t, bias_in[:, None])
    sums = lax.all_to_all(sums, "tile", 0, 0)
    entries = float(rows * tiles * width * (channels // GROUPS))

    def decode_body(*refs):
        decode_kernel(width, entries, tiles, *refs)

    return pl.pallas_call(
        decode_body,
        out_shape=jax.ShapeDtypeStruct((2, rows, width, channels), BF16),
        in_specs=[SMEM] + [VMEM] * 5,
        out_specs=VMEM,
        scratch_shapes=[pltpu.VMEM((4, 4, 3, channels, LANES), BF16)],
        compiler_params=PARAMS,
        name="decode",
    )(lengths, sums, hidden, w_mid_t, norm_gain[:, None], bias_mid[:, None])


def solution(mesh):
    return jax.shard_map(
        body,
        mesh=mesh,
        in_specs=(P("tm", "tile", None), P(), P(), P(), P(), P(), P(), P()),
        out_specs=P("tm", "tile", None, None),
        check_vma=False,
    )
```

time: 284 us -> 67 us (0.24); the launches traced: 280 us -> 66.3 us
  local copies, waits for them, and re-layouts: 187 us -> 10.9 us
  other arithmetic: 27.9 us -> 0 us
  matrix products: 17.4 us -> 0 us
  Pallas kernels: 0 us -> 9.19 us
    another operation x62 -> x0, local copies, waits for them, and re-layouts: 94.4 us -> none  [the longest x60 94.2 us: convolve(): patches = jnp.stack(taps, axis=3).reshape(frames * rows * width, 9, -1)]
    slice x32 -> x0, local copies, waits for them, and re-layouts: 42.4 us -> none  [the longest x30 40.6 us: convolve(): taps.append(planes[:, dy:dy + rows, dx:dx + width])]
    unnamed x125 -> x16, local copies, waits for them, and re-layouts: 42.1 us -> 7.8 us
    dot_general x7 -> x0, matrix products: 17.4 us -> none  [the longest x6 16.5 us: convolve(): jnp.einsum('ckn,nko->co', patches, weight[:, 9 * k:9 * k + 9, :], preferr...]
    mul x3 -> x0, other arithmetic: 14.3 us -> none  [convolve(): padded[i + k] * usable[i, k]]
    pallas_call x0 -> x3, Pallas kernels: none -> 9.19 us  [the longest x1 5.24 us: body(): pl.pallas_call(decode_body, out_shape=jax.ShapeDtypeStruct((2, rows, widt...]
    another operation x7 -> x0, other arithmetic: 8.96 us -> none  [the longest x6 8.78 us: convolve(): jnp.stack([padded[i + k] * usable[i, k] for i in range(frames)], axis=0)]
    convert_element_type x2 -> x0, local copies, waits for them, and re-layouts: 4.01 us -> none  [the longest x1 3.11 us: body(): hidden_f = hidden.astype(jnp.float32)]
  transfers between devices with their start and end apart: 3 -> 3, of which waited for: 1 -> 1; matrix products, arithmetic and copies ran while one was open for 2% -> 9% of each run, Pallas kernels for 0% -> 0%
where the time goes in v2:
time: 67 us; the launch traced here: 66.3 us
  blocking collectives  22.4 us (33%)
  starting transfers between devices  19 us (28%)
  local copies, waits for them, and re-layouts  10.9 us (16%)
  Pallas kernels  9.19 us (14%)
  waiting for transfers between devices  4.68 us (7%)
    all_gather x1, blocking collectives, body(): gathered = lax.all_gather(lt, 'tm', axis=0, tiled=True)  22.4 us
    all_to_all x1, starting transfers between devices, body(): sums = lax.all_to_all(sums, 'tile', 0, 0)  13.7 us
    unnamed x16, local copies, waits for them, and re-layouts  7.8 us
    pallas_call x1, Pallas kernels, body(): pl.pallas_call(decode_body, out_shape=jax.ShapeDtypeStruct((2, rows, widt...  5.24 us
    all_to_all x1, waiting for transfers between devices, body(): sums = lax.all_to_all(sums, 'tile', 0, 0)  4.67 us
    ppermute x1, starting transfers between devices, body(): above = lax.ppermute(picked, 'tile', [(i, i + 1) for i in range(tiles - 1)])  3.99 us
    pallas_call x1, Pallas kernels, body(): pl.pallas_call(hidden_body, out_shape=[jax.ShapeDtypeStruct((4, 4, channe...  2.93 us
  transfers between devices with their start and end apart: 3, of which 1 were waited for; matrix products, arithmetic and copies ran while one was open for 9% of the time, Pallas kernels for 0%

profile of v2, /device:TPU:1, one launch (start us, length us, event | category | flops | bytes accessed | tf_op | source)
XLA Modules:
  0.0 66.3 jit_solution(3367339622241037924)
XLA Ops:
  0.0 0.0 copy-start.5
  0.0 0.0 copy-start.6
  0.0 0.9 %reshape.9 = bf16[2,2,160,16]{3,2,1,0:T(8,128)(2,1)S(1)} reshape(bf16[2,2,2560]{2,1,0:T(2,128)(2,1)} %param.8) | data formatting | bytes 40960 | tf_op jit(solution)/shard_map/reshape | solution.py:150
  0.9 0.1 copy.23
  1.1 22.4 %all_gather.3.gathered_ref = bf16[32,2,16,256]{3,2,1,0:T(8,128)(2,1)S(1)} all-gather(bf16[2,2,16,256]{3,2,1,0:T(8,128)(2,1)S(1)} %pad.4.clone), channel_id=1, replica_groups=mesh['tm'=16,'tile'=32] {'tm'}, dimensions={0}, use_global_device_ids=true | all-gather | bytes 557056 | tf_op jit(solution)/shard_map/all_gather | solution.py:152
  23.5 0.0 copy-start.4
  23.5 0.7 copy-done.4
  24.2 1.0 %pick.1.refs_2_ = bf16[6,2,16,256]{3,2,1,0:T(8,128)(2,1)S(1)} custom-call(s32[32]{0:T(128)S(1)} %copy-done.4, bf16[32,2,16,256]{3,2,1,0:T(8,128)(2,1)S(1)} %all_gather.3.gathered_ref), custom_call_target="tpu_custom_call" | custom-call | tf_op jit(solution)/shard_map/pick/pallas_call | solution.py:153
  25.2 1.3 %collective-permute-start.1 = (bf16[6,2,16,256]{3,2,1,0:T(8,128)(2,1)S(1)}, bf16[6,2,16,256]{3,2,1,0:T(8,128)(2,1)S(1)}, u32[]{:S(2)}, u32[]{:S(2)}) collective-permute-start(bf16[6,2,16,256]{3,2,1,0:T(8,128)(2,1)S(1)} %pick.1.refs_2_), channel_id=1, source_target_pairs={{1,0},{2,1},{3,2},{4,3},{5,4},{6,5},{7,6},{8,7},{9,8},{10,9},{11,1... | collective-permute-start | bytes 294920 | tf_op jit(solution)/shard_map/ppermute | solution.py:162
  26.5 4.0 %collective-permute-start = (bf16[6,2,16,256]{3,2,1,0:T(8,128)(2,1)S(1)}, bf16[6,2,16,256]{3,2,1,0:T(8,128)(2,1)S(1)}, u32[]{:S(2)}, u32[]{:S(2)}) collective-permute-start(bf16[6,2,16,256]{3,2,1,0:T(8,128)(2,1)S(1)} %pick.1.refs_2_), channel_id=1, source_target_pairs={{0,1},{1,2},{2,3},{3,4},{4,5},{5,6},{6,7},{7,8},{8,9},{9,10},{10,1... | collective-permute-start | bytes 294920 | tf_op jit(solution)/shard_map/ppermute | solution.py:161
  30.5 0.8 %copy.19.refs_5_ = f32[192,1]{1,0:T(8,128)S(1)} copy(f32[192,1]{0,1:T(1,128)} %bitcast.13) | data formatting | bytes 1536 | tf_op jit(solution)/shard_map/broadcast_in_dim | solution.py:180
  31.3 1.1 %copy.18.refs_4_ = bf16[3,192,144]{2,1,0:T(8,128)(2,1)S(1)} copy(bf16[3,192,144]{1,2,0:T(8,128)(2,1)} %bitcast.12) | data formatting | bytes 331776 | tf_op jit(solution)/shard_map/reshape | solution.py:163
  32.4 0.0 collective-permute-done.1.refs_3_
  32.4 0.0 collective-permute-done.refs_1_
  32.4 0.0 copy-start.2
  32.4 0.6 copy-done.2
  33.1 2.9 %hidden.1 = (bf16[4,4,192,256]{3,2,1,0:T(8,128)(2,1)S(1)}, f32[32,2,128]{2,1,0:T(2,128)}) custom-call(s32[4]{0:T(128)S(1)} %copy-done.2, bf16[6,2,16,256]{3,2,1,0:T(8,128)(2,1)S(1)} %collective-permute-done.refs_1_, bf16[6,2,16,256]{3,2,1,0:T(8,128)(2,1)S(1)} %pick.1.refs_2_, bf16[6,2,16,256]{3,2,1,0:T(8,128)(2,1)S(1)} %collective-permute-done.1.refs_3_, ...), custom_call_target="tpu_custom_call" | custom-call | tf_op jit(solution)/shard_map/hidden/pallas_call | solution.py:169
  36.0 0.0 copy-start
  36.0 1.1 %copy-done = bf16[4,4,192,256]{3,2,1,0:T(8,128)(2,1)} copy-done((bf16[4,4,192,256]{3,2,1,0:T(8,128)(2,1)}, bf16[4,4,192,256]{3,2,1,0:T(8,128)(2,1)S(1)}, u32[]{:S(2)}) %copy-start) | copy-done | bytes 1572888
  37.2 13.7 %all-to-all-start = ((f32[32,2,128]{2,1,0:T(2,128)}), f32[32,2,128]{2,1,0:T(2,128)S(1)}, u32[]{:S(2)}, u32[]{:S(2)}) async-start(f32[32,2,128]{2,1,0:T(2,128)} %get-tuple-element.7), calls=%async_computation | async-start | bytes 65536 | tf_op jit(solution)/shard_map/all_to_all | solution.py:181
  50.9 0.0 copy-done.5
  50.9 0.1 copy.21.refs_4_
  51.0 0.0 copy-done.6
  51.0 0.1 copy.22.refs_5_
  51.2 0.0 copy-start.3
  51.2 3.8 %copy.20 = bf16[192,27,192]{0,2,1:T(8,128)(2,1)S(1)} copy(bf16[192,27,192]{2,0,1:T(8,128)(2,1)} %param.14) | data formatting | bytes 3981312 | tf_op args[6]
  55.0 4.7 %all-to-all-done.refs_1_ = f32[32,2,128]{2,1,0:T(2,128)S(1)} async-done(((f32[32,2,128]{2,1,0:T(2,128)}), f32[32,2,128]{2,1,0:T(2,128)S(1)}, u32[]{:S(2)}, u32[]{:S(2)}) %all-to-all-start) | async-done | bytes 32800 | tf_op jit(solution)/shard_map/all_to_all | solution.py:181
  59.7 0.0 copy-done.3
  59.7 0.0 copy-start.1
  59.7 1.4 %copy-done.1 = bf16[4,4,192,256]{3,2,1,0:T(8,128)(2,1)S(1)} copy-done((bf16[4,4,192,256]{3,2,1,0:T(8,128)(2,1)S(1)}, bf16[4,4,192,256]{3,2,1,0:T(8,128)(2,1)}, u32[]{:S(2)}) %copy-start.1) | copy-done | bytes 1572888
  61.1 5.2 %decode.1 = bf16[2,2,160,192]{3,2,1,0:T(8,128)(2,1)} custom-call(s32[4]{0:T(128)S(1)} %copy-done.3, f32[32,2,128]{2,1,0:T(2,128)S(1)} %all-to-all-done.refs_1_, bf16[4,4,192,256]{3,2,1,0:T(8,128)(2,1)S(1)} %copy-done.1, bf16[27,192,192]{2,1,0:T(8,128)(2,1)S(1)} %bitcast.10, f32[192,1]{1,0:T(8,128)S(1)} %copy.21.refs_4_, f32[192,1]{1,0:T(8,128)S(1)} %copy.22.refs_5_), custom_call_target="tpu_custom_call" | custom-call | tf_op jit(solution)/shard_map/decode/pallas_call | solution.py:187
  (1 shorter events, 0.0 us)
Async XLA Ops:
  0.0 50.9 %copy-start.5 = (f32[192]{0:T(256)S(1)}, f32[192]{0:T(256)}, u32[]{:S(2)}) copy-start(f32[192]{0:T(256)} %param.13) | copy-start | bytes 2308
  0.0 51.0 %copy-start.6 = (f32[192]{0:T(256)S(1)}, f32[192]{0:T(256)}, u32[]{:S(2)}) copy-start(f32[192]{0:T(256)} %param.15) | copy-start | bytes 2308
  23.5 0.7 copy-start.4
  25.2 7.2 %collective-permute-start.1 = (bf16[6,2,16,256]{3,2,1,0:T(8,128)(2,1)S(1)}, bf16[6,2,16,256]{3,2,1,0:T(8,128)(2,1)S(1)}, u32[]{:S(2)}, u32[]{:S(2)}) collective-permute-start(bf16[6,2,16,256]{3,2,1,0:T(8,128)(2,1)S(1)} %pick.1.refs_2_), channel_id=1, source_target_pairs={{1,0},{2,1},{3,2},{4,3},{5,4},{6,5},{7,6},{8,7},{9,8},{10,9},{11,1... | collective-permute-start | bytes 294920 | tf_op jit(solution)/shard_map/ppermute | solution.py:162
  26.5 5.9 %collective-permute-start = (bf16[6,2,16,256]{3,2,1,0:T(8,128)(2,1)S(1)}, bf16[6,2,16,256]{3,2,1,0:T(8,128)(2,1)S(1)}, u32[]{:S(2)}, u32[]{:S(2)}) collective-permute-start(bf16[6,2,16,256]{3,2,1,0:T(8,128)(2,1)S(1)} %pick.1.refs_2_), channel_id=1, source_target_pairs={{0,1},{1,2},{2,3},{3,4},{4,5},{5,6},{6,7},{7,8},{8,9},{9,10},{10,1... | collective-permute-start | bytes 294920 | tf_op jit(solution)/shard_map/ppermute | solution.py:161
  32.4 0.7 copy-start.2
  36.0 1.2 %copy-start = (bf16[4,4,192,256]{3,2,1,0:T(8,128)(2,1)}, bf16[4,4,192,256]{3,2,1,0:T(8,128)(2,1)S(1)}, u32[]{:S(2)}) copy-start(bf16[4,4,192,256]{3,2,1,0:T(8,128)(2,1)S(1)} %get-tuple-element.8.refs_2_) | copy-start | bytes 4718596
  37.2 22.5 %all-to-all-start = ((f32[32,2,128]{2,1,0:T(2,128)}), f32[32,2,128]{2,1,0:T(2,128)S(1)}, u32[]{:S(2)}, u32[]{:S(2)}) async-start(f32[32,2,128]{2,1,0:T(2,128)} %get-tuple-element.7), calls=%async_computation | async-start | bytes 65536 | tf_op jit(solution)/shard_map/all_to_all | solution.py:181
  51.2 8.5 %copy-start.3 = (s32[4]{0:T(128)S(1)}, s32[4]{0:T(128)}, u32[]{:S(2)}) copy-start(s32[4]{0:T(128)} %refs_0_.3) | copy-start | bytes 52
  59.7 1.4 %copy-start.1 = (bf16[4,4,192,256]{3,2,1,0:T(8,128)(2,1)S(1)}, bf16[4,4,192,256]{3,2,1,0:T(8,128)(2,1)}, u32[]{:S(2)}) copy-start(bf16[4,4,192,256]{3,2,1,0:T(8,128)(2,1)} %copy-done) | copy-start | bytes 4718596

commit v3 on v1

v3 whole, which is shorter than its diff:
```python
import jax
import jax.numpy as jnp
from jax import lax
from jax.experimental import pallas as pl
from jax.experimental.pallas import tpu as pltpu
from jax.sharding import PartitionSpec as P

GROUPS = 32
LANES = 256
EARLY = 13
VMEM = pl.BlockSpec(memory_space=pltpu.VMEM)
SMEM = pl.BlockSpec(memory_space=pltpu.SMEM)
HBM = pl.BlockSpec(memory_space=pltpu.HBM)
F32 = jnp.float32
BF16 = jnp.bfloat16
PARAMS = pltpu.CompilerParams(vmem_limit_bytes=40 * 1024 * 1024)


def roll_both(v, axis):
    return pltpu.roll(v, 1, axis), pltpu.roll(v, v.shape[axis] - 1, axis)


def split3(x):
    a = x.astype(BF16).astype(F32)
    b = (x - a).astype(BF16).astype(F32)
    return [a, b, (x - a - b).astype(BF16).astype(F32)]


def pick_kernel(zc, frames, whole_ref, gathered_ref, picked_ref, flags_ref, raw_ref):
    first = 2 * lax.axis_index("tm")
    base = first - 4
    raw_ref[...] = jnp.zeros_like(raw_ref)

    @pl.loop(0, frames)
    def _(p):
        j = whole_ref[p] - base

        @pl.when((j >= 0) & (j < 6))
        def _():
            raw_ref[j] = gathered_ref[p].astype(F32)

    row = lax.broadcasted_iota(jnp.int32, (16, 128), 0)
    lane = lax.broadcasted_iota(jnp.int32, (16, 128), 1)
    channel = jnp.where(lax.rem(lane, zc) == row, 1.0, 0.0).astype(BF16)
    own = lane // zc == lax.rem(row, 128 // zc)
    rows, cells = raw_ref.shape[1:]
    empty = jnp.zeros((LANES - cells // zc, 128), BF16)
    for f in range(6):
        for r in range(rows):
            blocks = []
            for b in range(0, cells, 256):
                halves = [
                    jnp.broadcast_to(raw_ref[f, r : r + 1, b + d : b + d + 128], (128 // zc, 128)) for d in (0, 128)
                ]
                blocks.append(jnp.where(own, jnp.concatenate(halves, axis=0), 0.0).astype(BF16))
            spread_out = jnp.concatenate(blocks + [empty], axis=0)
            picked_ref[f, r] = lax.dot_general(
                channel, spread_out, (((1,), (1,)), ((), ())), preferred_element_type=F32
            ).astype(BF16)

    for j in range(4):
        frame = first - 2 + j
        begin = jnp.int32(0)
        end = jnp.int32(0)
        for r in range(frames, whole_ref.shape[0]):
            end = end + whole_ref[r]
            begin = jnp.where(end <= frame, end, begin)
        for k in range(2):
            flag = jnp.where(frame - 2 + k >= begin, 1.0, 0.0).astype(F32)
            flags_ref[2 * j + k : 2 * j + k + 1, :] = jnp.full((1, LANES), flag, F32)


def group_mask(channels, frame):
    per_group = channels // GROUPS
    channel = lax.broadcasted_iota(jnp.int32, (channels, 128), 0)
    lane = lax.broadcasted_iota(jnp.int32, (channels, 128), 1) - GROUPS * frame
    low = lane * per_group
    return (channel >= low) & (channel < low + per_group) & (lane >= 0) & (lane < GROUPS)


def spread(xs_ref, f, e, v):
    left, right = roll_both(v.astype(F32), 1)
    xs_ref[f, e, 0:16] = left.astype(BF16)
    xs_ref[f, e, 16:32] = v
    xs_ref[f, e, 32:48] = right.astype(BF16)


def frame_weights(w_ref, flags_ref):
    channels = w_ref.shape[1]
    taps = w_ref.shape[0] - 8
    parts = [w_ref[:taps]] + split3(w_ref[taps : taps + 1]) + [jnp.zeros((13, channels), F32)]
    whole = jnp.concatenate(parts, axis=0).T
    lane = lax.broadcasted_iota(jnp.int32, (1, whole.shape[1]), 1)
    result = []
    for j in range(4):
        u0 = flags_ref[2 * j : 2 * j + 1, 0:1]
        u1 = flags_ref[2 * j + 1 : 2 * j + 2, 0:1]
        keep = jnp.where(lane < 144, u0, jnp.where(lane < 288, u1, 1.0))
        result.append((whole * keep).astype(BF16))
    return result


def hidden_t(weights, xs_ref, j, r):
    patches = [xs_ref[j + k, r : r + 3].reshape(144, LANES) for k in range(3)]
    patches.append(jnp.ones((16, LANES), BF16))
    return jnp.dot(weights, jnp.concatenate(patches, axis=0), preferred_element_type=F32)


def sums_kernel(width, tiles, flags_ref, above_ref, picked_ref, w_ref, sums_ref, xs_ref, s1_ref, s2_ref):
    channels = w_ref.shape[1]
    tile = lax.axis_index("tile")
    for f in range(6):
        for e in range(4):
            spread(xs_ref, f, e, (above_ref, picked_ref)[e // 2][f, e % 2])
        xs_ref[f, 4] = jnp.zeros((48, LANES), BF16)
    weights = frame_weights(w_ref, flags_ref)
    lane = lax.broadcasted_iota(jnp.int32, (channels, LANES), 1)
    limit = jnp.where(tile > 0, width, 0)

    def row(j, r):
        h = hidden_t(weights[j], xs_ref, j, r)
        h = jnp.where(lane < (limit if r == 0 else width), h.astype(BF16).astype(F32), 0.0)
        return h[:, :128] + h[:, 128:], h[:, :128] * h[:, :128] + h[:, 128:] * h[:, 128:]

    for j in range(4):
        a1, a2 = row(j, 0)
        b1, b2 = row(j, 1)
        s1_ref[j] = a1 + b1
        s2_ref[j] = a2 + b2

    @pl.when(tile == tiles - 1)
    def _():
        for j in range(4):
            c1, c2 = row(j, 2)
            s1_ref[j] = s1_ref[j] + c1
            s2_ref[j] = s2_ref[j] + c2

    d1 = jnp.zeros((channels, 128), F32)
    d2 = jnp.zeros((channels, 128), F32)
    for j in range(4):
        mask = group_mask(channels, j)
        d1 = jnp.where(mask, jnp.sum(s1_ref[j], axis=1, keepdims=True), d1)
        d2 = jnp.where(mask, jnp.sum(s2_ref[j], axis=1, keepdims=True), d2)
    block = jnp.concatenate([jnp.sum(d1, axis=0, keepdims=True), jnp.sum(d2, axis=0, keepdims=True)], axis=0)
    sums_ref[...] = jnp.broadcast_to(block[None], sums_ref.shape)


def hidden_kernel(
    width, flags_ref, above_ref, picked_ref, below_ref, w_ref, w_mid_hbm, hidden_ref, early_ref, xs_ref, sem
):
    fetch = pltpu.make_async_copy(w_mid_hbm.at[0:EARLY], early_ref, sem)
    fetch.start()
    for f in range(6):
        for e in range(6):
            spread(xs_ref, f, e, (above_ref, picked_ref, below_ref)[e // 2][f, e % 2])
    weights = frame_weights(w_ref, flags_ref)
    for j in range(4):
        for r in range(4):
            hidden_ref[j, r] = hidden_t(weights[j], xs_ref, j, r).T[:width].astype(BF16)
    fetch.wait()


def decode_kernel(
    entries, tiles, flags_ref, sums_ref, h_ref, early_ref, w_hbm, gain_ref, bias_ref, out_ref, act_ref, acc_ref, late_ref, sem
):
    middle = pltpu.make_async_copy(w_hbm.at[EARLY:18], late_ref.at[0 : 18 - EARLY], sem.at[0])
    last = pltpu.make_async_copy(w_hbm.at[18:27], late_ref.at[18 - EARLY : 27 - EARLY], sem.at[1])
    middle.start()
    last.start()
    width, channels = h_ref.shape[2:]
    per_group = channels // GROUPS
    tile = lax.axis_index("tile")
    total = jnp.sum(sums_ref[...], axis=0)
    average = total[0:1] / entries
    variance = total[1:2] / entries - average * average
    rstd = lax.rsqrt(variance + 1e-06)
    packed = jnp.concatenate(split3(average) + split3(rstd) + [jnp.zeros((2, 128), F32)], axis=0).astype(BF16)
    source = lax.broadcasted_iota(jnp.int32, (128, LANES), 0)
    channel = lax.broadcasted_iota(jnp.int32, (128, LANES), 1)
    position = lax.broadcasted_iota(jnp.int32, (width, channels), 0)
    half_gain = 0.5 * gain_ref[...]
    bias = bias_ref[...]
    for j in range(4):
        start = per_group * (source - GROUPS * j)
        expand = (channel >= start) & (channel < start + per_group) & (source >= GROUPS * j) & (source < GROUPS * (j + 1))
        wide = jnp.dot(packed, jnp.where(expand, 1.0, 0.0).astype(BF16), preferred_element_type=F32)
        mean = (wide[0:1] + wide[1:2] + wide[2:3])[:, :channels]
        scale = (wide[3:4] + wide[4:5] + wide[5:6])[:, :channels] * half_gain
        for r in range(4):
            u = (h_ref[j, r].astype(F32) - mean) * scale
            a = u + u * jnp.tanh(u)
            if r == 0:
                a = jnp.where(tile > 0, a, 0.0)
            if r == 3:
                a = jnp.where(tile < tiles - 1, a, 0.0)
            left, right = roll_both(a, 0)
            act_ref[j, r, 0] = jnp.where(position > 0, left, 0.0).astype(BF16)
            act_ref[j, r, 1] = a.astype(BF16)
            act_ref[j, r, 2] = jnp.where(position < width - 1, right, 0.0).astype(BF16)
        for i in range(2):
            k = j - i
            if k < 0 or k > 2:
                continue
            if i == 0 and k > 0:
                (middle if k == 1 else last).wait()
            taps = [early_ref[t] if t < EARLY else late_ref[t - EARLY] for t in range(9 * k, 9 * k + 9)]
            for r in range(2):
                term = None
                for dy in range(3):
                    for dx in range(3):
                        d = jnp.dot(act_ref[j, r + dy, dx], taps[3 * dy + dx], preferred_element_type=F32)
                        term = d if term is None else term + d
                if k < 2:
                    flag = flags_ref[2 * (i + 2) + k : 2 * (i + 2) + k + 1, :channels]
                    term = jnp.where(flag > 0.0, term, 0.0)
                if k == 0:
                    acc_ref[i, r] = term
                elif k == 1:
                    acc_ref[i, r] = acc_ref[i, r] + term
                else:
                    y = acc_ref[i, r] + term + bias + h_ref[2 + i, r + 1].astype(F32)
                    out_ref[i, r] = y.astype(BF16)


def body(latents, frame_slot, lengths, w_in, bias_in, norm_gain, w_mid, bias_mid):
    rows = latents.shape[1]
    zc = w_in.shape[0]
    channels = w_in.shape[2]
    width = latents.shape[2] // zc
    tiles = lax.axis_size("tile")
    whole = jnp.concatenate([frame_slot, lengths])
    latents, whole = lax.optimization_barrier((latents, whole))
    gathered = lax.all_gather(latents, "tm", axis=0, tiled=True)

    def pick_body(*refs):
        pick_kernel(zc, frame_slot.shape[0], *refs)

    picked, flags = pl.pallas_call(
        pick_body,
        out_shape=[jax.ShapeDtypeStruct((6, rows, zc, LANES), BF16), jax.ShapeDtypeStruct((8, LANES), F32)],
        in_specs=[SMEM, VMEM],
        out_specs=[VMEM, VMEM],
        scratch_shapes=[
            pltpu.VMEM((6,) + latents.shape[1:], F32),
        ],
        compiler_params=PARAMS,
        name="pick",
    )(whole, gathered)
    above = lax.ppermute(picked, "tile", [(i, i + 1) for i in range(tiles - 1)])
    below = lax.ppermute(picked, "tile", [(i + 1, i) for i in range(tiles - 1)])
    w_in = jnp.transpose(w_in, (1, 0, 2)).reshape(27 * zc, channels).astype(F32)
    w_in = jnp.concatenate([w_in, jnp.broadcast_to(bias_in[None], (8, channels))], axis=0)
    w_mid = jnp.transpose(w_mid, (1, 0, 2))

    def sums_body(*refs):
        sums_kernel(width, tiles, *refs)

    def hidden_body(*refs):
        hidden_kernel(width, *refs)

    sums = pl.pallas_call(
        sums_body,
        out_shape=jax.ShapeDtypeStruct((tiles, 2, 128), F32),
        in_specs=[VMEM] * 4,
        out_specs=VMEM,
        scratch_shapes=[
            pltpu.VMEM((6, 5, 3 * zc, LANES), BF16),
            pltpu.VMEM((4, channels, 128), F32),
            pltpu.VMEM((4, channels, 128), F32),
        ],
        compiler_params=PARAMS,
        name="sums",
    )(flags, above, picked, w_in)
    sums = lax.all_to_all(sums, "tile", 0, 0)
    hidden, early = pl.pallas_call(
        hidden_body,
        out_shape=[
            jax.ShapeDtypeStruct((4, 4, width, channels), BF16),
            jax.ShapeDtypeStruct((EARLY, channels, channels), BF16),
        ],
        in_specs=[VMEM] * 5 + [HBM],
        out_specs=[VMEM, VMEM],
        scratch_shapes=[
            pltpu.VMEM((6, 6, 3 * zc, LANES), BF16),
            pltpu.SemaphoreType.DMA,
        ],
        compiler_params=pltpu.CompilerParams(vmem_limit_bytes=50000 * 1024),
        cost_estimate=pl.CostEstimate(flops=4_000_000_000, bytes_accessed=2_000_000, transcendentals=0),
        name="hidden",
    )(flags, above, picked, below, w_in, w_mid)
    entries = float(rows * tiles * width * (channels // GROUPS))

    def decode_body(*refs):
        decode_kernel(entries, tiles, *refs)

    return pl.pallas_call(
        decode_body,
        out_shape=jax.ShapeDtypeStruct((2, rows, width, channels), BF16),
        in_specs=[VMEM, VMEM, VMEM, VMEM, HBM, VMEM, VMEM],
        out_specs=VMEM,
        scratch_shapes=[
            pltpu.VMEM((4, 4, 3, width, channels), BF16),
            pltpu.VMEM((2, 2, width, channels), F32),
            pltpu.VMEM((27 - EARLY, channels, channels), BF16),
            pltpu.SemaphoreType.DMA((2,)),
        ],
        compiler_params=pltpu.CompilerParams(vmem_limit_bytes=52000 * 1024),
        name="decode",
    )(flags, sums, hidden, early, w_mid, norm_gain[None, :], bias_mid[None, :])


def solution(mesh):
    return jax.shard_map(
        body,
        mesh=mesh,
        in_specs=(P("tm", "tile", None), P(), P(), P(), P(), P(), P(), P()),
        out_specs=P("tm", "tile", None, None),
        check_vma=False,
    )
```

time: 284 us -> 58.3 us (0.21); the launches traced: 280 us -> 58 us
  local copies, waits for them, and re-layouts: 187 us -> 0.02 us
  other arithmetic: 27.9 us -> 1.77 us
  matrix products: 17.4 us -> 0 us
  Pallas kernels: 0 us -> 9.44 us
    another operation x62 -> x0, local copies, waits for them, and re-layouts: 94.4 us -> none  [the longest x60 94.2 us: convolve(): patches = jnp.stack(taps, axis=3).reshape(frames * rows * width, 9, -1)]
    slice x32 -> x0, local copies, waits for them, and re-layouts: 42.4 us -> none  [the longest x30 40.6 us: convolve(): taps.append(planes[:, dy:dy + rows, dx:dx + width])]
    unnamed x125 -> x6, local copies, waits for them, and re-layouts: 42.1 us -> 0.02 us
    dot_general x7 -> x0, matrix products: 17.4 us -> none  [the longest x6 16.5 us: convolve(): jnp.einsum('ckn,nko->co', patches, weight[:, 9 * k:9 * k + 9, :], preferr...]
    mul x3 -> x0, other arithmetic: 14.3 us -> none  [convolve(): padded[i + k] * usable[i, k]]
    pallas_call x0 -> x4, Pallas kernels: none -> 9.44 us  [the longest x1 4.84 us: body(): pl.pallas_call(decode_body, out_shape=jax.ShapeDtypeStruct((2, rows, widt...]
    another operation x7 -> x0, other arithmetic: 8.96 us -> none  [the longest x6 8.78 us: convolve(): jnp.stack([padded[i + k] * usable[i, k] for i in range(frames)], axis=0)]
    convert_element_type x2 -> x0, local copies, waits for them, and re-layouts: 4.01 us -> none  [the longest x1 3.11 us: body(): hidden_f = hidden.astype(jnp.float32)]
  transfers between devices with their start and end apart: 3 -> 3, of which waited for: 1 -> 1; matrix products, arithmetic and copies ran while one was open for 2% -> 2% of each run, Pallas kernels for 0% -> 6%
where the time goes in v3:
time: 58.3 us; the launch traced here: 58 us
  blocking collectives  22 us (38%)
  starting transfers between devices  17.4 us (30%)
  Pallas kernels  9.44 us (16%)
  waiting for transfers between devices  7.28 us (12%)
  other arithmetic  1.77 us (3%)
    all_gather x1, blocking collectives, body(): gathered = lax.all_gather(latents, 'tm', axis=0, tiled=True)  22 us
    all_to_all x1, starting transfers between devices, body(): sums = lax.all_to_all(sums, 'tile', 0, 0)  14.1 us
    all_to_all x1, waiting for transfers between devices, body(): sums = lax.all_to_all(sums, 'tile', 0, 0)  7.27 us
    pallas_call x1, Pallas kernels, body(): pl.pallas_call(decode_body, out_shape=jax.ShapeDtypeStruct((2, rows, widt...  4.84 us
    ppermute x1, starting transfers between devices, body(): above = lax.ppermute(picked, 'tile', [(i, i + 1) for i in range(tiles - 1)])  2.02 us
    pallas_call x1, Pallas kernels, body(): pl.pallas_call(sums_body, out_shape=jax.ShapeDtypeStruct((tiles, 2, 128),...  1.76 us
    pallas_call x1, Pallas kernels, body(): pl.pallas_call(hidden_body, out_shape=[jax.ShapeDtypeStruct((4, 4, width,...  1.45 us
    pallas_call x1, Pallas kernels, body(): pl.pallas_call(pick_body, out_shape=[jax.ShapeDtypeStruct((6, rows, zc, L...  1.39 us
  transfers between devices with their start and end apart: 3, of which 1 were waited for; matrix products, arithmetic and copies ran while one was open for 2% of the time, Pallas kernels for 6%

profile of v3, /device:TPU:1, one launch (start us, length us, event | category | flops | bytes accessed | tf_op | source)
XLA Modules:
  0.0 58.0 jit_solution(2568407446742140051)
XLA Ops:
  0.0 0.0 copy-start.2
  0.0 0.8 %pad_add_fusion.refs_0_ = s32[36]{0:T(128)S(1)} fusion(s32[4]{0:T(128)} %param.10, s32[32]{0:T(128)} %param.9), kind=kLoop, calls=%fused_computation.1 | loop fusion | flops 36 | bytes 288 | tf_op jit(solution)/shard_map/concatenate | solution.py:231
  0.8 22.0 %all_gather.3.refs_1_ = bf16[32,2,2560]{2,1,0:T(2,128)(2,1)S(1)} all-gather(bf16[2,2,2560]{2,1,0:T(2,128)(2,1)} %param.8), channel_id=1, replica_groups=mesh['tm'=16,'tile'=32] {'tm'}, dimensions={0}, use_global_device_ids=true | all-gather | bytes 348160 | tf_op jit(solution)/shard_map/all_gather | solution.py:233
  22.8 1.4 %pick.1 = (bf16[6,2,16,256]{3,2,1,0:T(8,128)(2,1)S(1)}, f32[8,256]{1,0:T(8,128)S(1)}) custom-call(s32[36]{0:T(128)S(1)} %pad_add_fusion.refs_0_, bf16[32,2,2560]{2,1,0:T(2,128)(2,1)S(1)} %all_gather.3.refs_1_), custom_call_target="tpu_custom_call" | custom-call | tf_op jit(solution)/shard_map/pick/pallas_call | solution.py:238
  24.2 2.0 %collective-permute-start = (bf16[6,2,16,256]{3,2,1,0:T(8,128)(2,1)S(1)}, bf16[6,2,16,256]{3,2,1,0:T(8,128)(2,1)S(1)}, u32[]{:S(2)}, u32[]{:S(2)}) collective-permute-start(bf16[6,2,16,256]{3,2,1,0:T(8,128)(2,1)S(1)} %get-tuple-element.14.refs_2_), channel_id=1, source_target_pairs={{0,1},{1,2},{2,3},{3,4},{4,5},{5,6},{6,7},{7,8},{8,9},{9,10},{10,1... | collective-permute-start | bytes 294920 | tf_op jit(solution)/shard_map/ppermute | solution.py:249
  26.2 1.3 %collective-permute-start.1 = (bf16[6,2,16,256]{3,2,1,0:T(8,128)(2,1)S(1)}, bf16[6,2,16,256]{3,2,1,0:T(8,128)(2,1)S(1)}, u32[]{:S(2)}, u32[]{:S(2)}) collective-permute-start(bf16[6,2,16,256]{3,2,1,0:T(8,128)(2,1)S(1)} %get-tuple-element.14.refs_2_), channel_id=1, source_target_pairs={{1,0},{2,1},{3,2},{4,3},{5,4},{6,5},{7,6},{8,7},{9,8},{10,9},{11,1... | collective-permute-start | bytes 294920 | tf_op jit(solution)/shard_map/ppermute | solution.py:250
  27.5 1.0 %convert_element_type.13 = f32[16,27,192]{2,0,1:T(8,128)S(1)} convert(bf16[16,27,192]{2,0,1:T(8,128)(2,1)} %param.11) | non-fusion elementwise | flops 82944 | bytes 497664 | tf_op jit(solution)/shard_map/convert_element_type | solution.py:251
  28.5 0.0 copy-done.2
  28.6 0.0 collective-permute-done.refs_1_
  28.6 1.8 %sums.1 = f32[32,2,128]{2,1,0:T(2,128)} custom-call(f32[8,256]{1,0:T(8,128)S(1)} %get-tuple-element.13.refs_0_, bf16[6,2,16,256]{3,2,1,0:T(8,128)(2,1)S(1)} %collective-permute-done.refs_1_, bf16[6,2,16,256]{3,2,1,0:T(8,128)(2,1)S(1)} %get-tuple-element.14.refs_2_, f32[440,192]{1,0:T(8,128)S(1)} %pad_maximum_fusion.refs_3_.refs_4_), custom_call_target="tpu_custom_call" | custom-call | tf_op jit(solution)/shard_map/sums/pallas_call | solution.py:261
  30.3 14.1 %all-to-all-start = ((f32[32,2,128]{2,1,0:T(2,128)}), f32[32,2,128]{2,1,0:T(2,128)S(1)}, u32[]{:S(2)}, u32[]{:S(2)}) async-start(f32[32,2,128]{2,1,0:T(2,128)} %sums.1), calls=%async_computation | async-start | bytes 65536 | tf_op jit(solution)/shard_map/all_to_all | solution.py:274
  44.4 0.0 collective-permute-done.1.refs_3_
  44.4 0.0 copy-start
  44.4 0.0 copy-start.1
  44.4 1.5 %hidden.1 = (bf16[4,4,160,192]{3,2,1,0:T(8,128)(2,1)S(1)}, bf16[13,192,192]{2,1,0:T(8,128)(2,1)S(1)}) custom-call(f32[8,256]{1,0:T(8,128)S(1)} %get-tuple-element.13.refs_0_, bf16[6,2,16,256]{3,2,1,0:T(8,128)(2,1)S(1)} %collective-permute-done.refs_1_, bf16[6,2,16,256]{3,2,1,0:T(8,128)(2,1)S(1)} %get-tuple-element.14.refs_2_, ...), custom_call_target="tpu_custom_call" | custom-call | flops 4000000000 | bytes 2000000 | tf_op jit(solution)/shard_map/hidden/pallas_call | solution.py:275
  45.9 7.3 %all-to-all-done.refs_1_ = f32[32,2,128]{2,1,0:T(2,128)S(1)} async-done(((f32[32,2,128]{2,1,0:T(2,128)}), f32[32,2,128]{2,1,0:T(2,128)S(1)}, u32[]{:S(2)}, u32[]{:S(2)}) %all-to-all-start) | async-done | bytes 32800 | tf_op jit(solution)/shard_map/all_to_all | solution.py:274
  53.2 0.0 copy-done
  53.2 0.0 copy-done.1
  53.2 4.8 %decode.1 = bf16[2,2,160,192]{3,2,1,0:T(8,128)(2,1)} custom-call(f32[8,256]{1,0:T(8,128)S(1)} %get-tuple-element.13.refs_0_, f32[32,2,128]{2,1,0:T(2,128)S(1)} %all-to-all-done.refs_1_, bf16[4,4,160,192]{3,2,1,0:T(8,128)(2,1)S(1)} %get-tuple-element.15.refs_2_, bf16[13,192,192]{2,1,0:T(8,128)(2,1)S(1)} %get-tuple-element.16.refs_3_, ...), custom_call_target="tpu_custom_call" | custom-call | tf_op jit(solution)/shard_map/decode/pallas_call | solution.py:296
  (2 shorter events, 0.0 us)
Async XLA Ops:
  0.0 28.5 %copy-start.2 = (f32[192]{0:T(256)S(1)}, f32[192]{0:T(256)}, u32[]{:S(2)}) copy-start(f32[192]{0:T(256)} %param.12) | copy-start | bytes 2308
  24.2 4.4 %collective-permute-start = (bf16[6,2,16,256]{3,2,1,0:T(8,128)(2,1)S(1)}, bf16[6,2,16,256]{3,2,1,0:T(8,128)(2,1)S(1)}, u32[]{:S(2)}, u32[]{:S(2)}) collective-permute-start(bf16[6,2,16,256]{3,2,1,0:T(8,128)(2,1)S(1)} %get-tuple-element.14.refs_2_), channel_id=1, source_target_pairs={{0,1},{1,2},{2,3},{3,4},{4,5},{5,6},{6,7},{7,8},{8,9},{9,10},{10,1... | collective-permute-start | bytes 294920 | tf_op jit(solution)/shard_map/ppermute | solution.py:249
  26.2 18.2 %collective-permute-start.1 = (bf16[6,2,16,256]{3,2,1,0:T(8,128)(2,1)S(1)}, bf16[6,2,16,256]{3,2,1,0:T(8,128)(2,1)S(1)}, u32[]{:S(2)}, u32[]{:S(2)}) collective-permute-start(bf16[6,2,16,256]{3,2,1,0:T(8,128)(2,1)S(1)} %get-tuple-element.14.refs_2_), channel_id=1, source_target_pairs={{1,0},{2,1},{3,2},{4,3},{5,4},{6,5},{7,6},{8,7},{9,8},{10,9},{11,1... | collective-permute-start | bytes 294920 | tf_op jit(solution)/shard_map/ppermute | solution.py:250
  30.3 22.8 %all-to-all-start = ((f32[32,2,128]{2,1,0:T(2,128)}), f32[32,2,128]{2,1,0:T(2,128)S(1)}, u32[]{:S(2)}, u32[]{:S(2)}) async-start(f32[32,2,128]{2,1,0:T(2,128)} %sums.1), calls=%async_computation | async-start | bytes 65536 | tf_op jit(solution)/shard_map/all_to_all | solution.py:274
  44.4 8.8 %copy-start = (f32[192]{0:T(256)S(1)}, f32[192]{0:T(256)}, u32[]{:S(2)}) copy-start(f32[192]{0:T(256)} %param.13) | copy-start | bytes 2308
  44.4 8.7 %copy-start.1 = (f32[192]{0:T(256)S(1)}, f32[192]{0:T(256)}, u32[]{:S(2)}) copy-start(f32[192]{0:T(256)} %param.15) | copy-start | bytes 2308

commit v4 on v3

--- a/solution.py
+++ b/solution.py
@@ -8,6 +8,8 @@
 GROUPS = 32
 LANES = 256
 EARLY = 13
+TIMES = list(range(15, -1, -1))
+TILES = [8 * x + z for z in (4, 5, 6, 7, 3, 2, 1, 0) for x in (2, 3, 1, 0)]
 VMEM = pl.BlockSpec(memory_space=pltpu.VMEM)
 SMEM = pl.BlockSpec(memory_space=pltpu.SMEM)
 HBM = pl.BlockSpec(memory_space=pltpu.HBM)
@@ -26,19 +28,14 @@
     return [a, b, (x - a - b).astype(BF16).astype(F32)]
 
 
-def pick_kernel(zc, frames, whole_ref, gathered_ref, picked_ref, flags_ref, raw_ref):
+def pick_kernel(zc, frames, whole_ref, gathered_ref, picked_ref, flags_ref, where_ref, raw_ref):
     first = 2 * lax.axis_index("tm")
-    base = first - 4
-    raw_ref[...] = jnp.zeros_like(raw_ref)
-
-    @pl.loop(0, frames)
-    def _(p):
-        j = whole_ref[p] - base
-
-        @pl.when((j >= 0) & (j < 6))
-        def _():
-            raw_ref[j] = gathered_ref[p].astype(F32)
-
+    for p in range(frames):
+        where_ref[whole_ref[p]] = 2 * TIMES.index(p // 2) + p % 2
+    for j in range(6):
+        t = first - 4 + j
+        raw = gathered_ref[where_ref[jnp.maximum(t, 0)]].astype(F32)
+        raw_ref[j] = raw if j > 3 else jnp.where(t >= 0, raw, 0.0)
     row = lax.broadcasted_iota(jnp.int32, (16, 128), 0)
     lane = lax.broadcasted_iota(jnp.int32, (16, 128), 1)
     channel = jnp.where(lax.rem(lane, zc) == row, 1.0, 0.0).astype(BF16)
@@ -86,41 +83,39 @@
 
 
 def frame_weights(w_ref, flags_ref):
-    channels = w_ref.shape[1]
-    taps = w_ref.shape[0] - 8
-    parts = [w_ref[:taps]] + split3(w_ref[taps : taps + 1]) + [jnp.zeros((13, channels), F32)]
-    whole = jnp.concatenate(parts, axis=0).T
-    lane = lax.broadcasted_iota(jnp.int32, (1, whole.shape[1]), 1)
+    taps = w_ref.shape[1] - 8
+    whole = w_ref[:, :taps].astype(BF16)
+    lane = lax.broadcasted_iota(jnp.int32, (1, taps), 1)
     result = []
     for j in range(4):
         u0 = flags_ref[2 * j : 2 * j + 1, 0:1]
         u1 = flags_ref[2 * j + 1 : 2 * j + 2, 0:1]
-        keep = jnp.where(lane < 144, u0, jnp.where(lane < 288, u1, 1.0))
-        result.append((whole * keep).astype(BF16))
-    return result
-
-
-def hidden_t(weights, xs_ref, j, r):
-    patches = [xs_ref[j + k, r : r + 3].reshape(144, LANES) for k in range(3)]
-    patches.append(jnp.ones((16, LANES), BF16))
-    return jnp.dot(weights, jnp.concatenate(patches, axis=0), preferred_element_type=F32)
+        keep = jnp.where(lane < taps // 3, u0, jnp.where(lane < 2 * taps // 3, u1, 1.0)).astype(BF16)
+        result.append(whole * keep)
+    return result, w_ref[:, taps : taps + 1]
+
+
+def hidden_t(weights, bias, xs_ref, j, r):
+    patches = jnp.concatenate([xs_ref[j + k, r : r + 3].reshape(144, LANES) for k in range(3)], axis=0)
+    return jnp.dot(weights, patches, preferred_element_type=F32) + bias
 
 
 def sums_kernel(width, tiles, flags_ref, above_ref, picked_ref, w_ref, sums_ref, xs_ref, s1_ref, s2_ref):
-    channels = w_ref.shape[1]
+    channels = w_ref.shape[0]
     tile = lax.axis_index("tile")
     for f in range(6):
         for e in range(4):
             spread(xs_ref, f, e, (above_ref, picked_ref)[e // 2][f, e % 2])
         xs_ref[f, 4] = jnp.zeros((48, LANES), BF16)
-    weights = frame_weights(w_ref, flags_ref)
-    lane = lax.broadcasted_iota(jnp.int32, (channels, LANES), 1)
-    limit = jnp.where(tile > 0, width, 0)
+    weights, bias = frame_weights(w_ref, flags_ref)
+    rest = lax.broadcasted_iota(jnp.int32, (channels, 128), 1) < width - 128
 
     def row(j, r):
-        h = hidden_t(weights[j], xs_ref, j, r)
-        h = jnp.where(lane < (limit if r == 0 else width), h.astype(BF16).astype(F32), 0.0)
-        return h[:, :128] + h[:, 128:], h[:, :128] * h[:, :128] + h[:, 128:] * h[:, 128:]
+        h = hidden_t(weights[j], bias, xs_ref, j, r).astype(BF16).astype(F32)
+        a, b = h[:, :128], jnp.where(rest, h[:, 128:], 0.0)
+        if r == 0:
+            a, b = jnp.where(tile > 0, a, 0.0), jnp.where(tile > 0, b, 0.0)
+        return a + b, a * a + b * b
 
     for j in range(4):
         a1, a2 = row(j, 0)
@@ -153,20 +148,18 @@
     for f in range(6):
         for e in range(6):
             spread(xs_ref, f, e, (above_ref, picked_ref, below_ref)[e // 2][f, e % 2])
-    weights = frame_weights(w_ref, flags_ref)
+    weights, bias = frame_weights(w_ref, flags_ref)
     for j in range(4):
         for r in range(4):
-            hidden_ref[j, r] = hidden_t(weights[j], xs_ref, j, r).T[:width].astype(BF16)
+            hidden_ref[j, r] = hidden_t(weights[j], bias, xs_ref, j, r).T[:width].astype(BF16)
     fetch.wait()
 
 
 def decode_kernel(
-    entries, tiles, flags_ref, sums_ref, h_ref, early_ref, w_hbm, gain_ref, bias_ref, out_ref, act_ref, acc_ref, late_ref, sem
+    entries, tiles, flags_ref, sums_ref, h_ref, early_ref, w_hbm, gain_ref, bias_ref, out_hbm, act_ref, acc_ref, late_ref, out_ref, sem, out_sem
 ):
-    middle = pltpu.make_async_copy(w_hbm.at[EARLY:18], late_ref.at[0 : 18 - EARLY], sem.at[0])
-    last = pltpu.make_async_copy(w_hbm.at[18:27], late_ref.at[18 - EARLY : 27 - EARLY], sem.at[1])
-    middle.start()
-    last.start()
+    late = pltpu.make_async_copy(w_hbm.at[EARLY:27], late_ref, sem)
+    late.start()
     width, channels = h_ref.shape[2:]
     per_group = channels // GROUPS
     tile = lax.axis_index("tile")
@@ -179,8 +172,10 @@
     channel = lax.broadcasted_iota(jnp.int32, (128, LANES), 1)
     position = lax.broadcasted_iota(jnp.int32, (width, channels), 0)
     half_gain = 0.5 * gain_ref[...]
+    results = []
     bias = bias_ref[...]
-    for j in range(4):
+
+    def activate(j):
         start = per_group * (source - GROUPS * j)
         expand = (channel >= start) & (channel < start + per_group) & (source >= GROUPS * j) & (source < GROUPS * (j + 1))
         wide = jnp.dot(packed, jnp.where(expand, 1.0, 0.0).astype(BF16), preferred_element_type=F32)
@@ -197,29 +192,41 @@
             act_ref[j, r, 0] = jnp.where(position > 0, left, 0.0).astype(BF16)
             act_ref[j, r, 1] = a.astype(BF16)
             act_ref[j, r, 2] = jnp.where(position < width - 1, right, 0.0).astype(BF16)
-        for i in range(2):
-            k = j - i
-            if k < 0 or k > 2:
-                continue
-            if i == 0 and k > 0:
-                (middle if k == 1 else last).wait()
-            taps = [early_ref[t] if t < EARLY else late_ref[t - EARLY] for t in range(9 * k, 9 * k + 9)]
-            for r in range(2):
-                term = None
-                for dy in range(3):
-                    for dx in range(3):
-                        d = jnp.dot(act_ref[j, r + dy, dx], taps[3 * dy + dx], preferred_element_type=F32)
-                        term = d if term is None else term + d
-                if k < 2:
-                    flag = flags_ref[2 * (i + 2) + k : 2 * (i + 2) + k + 1, :channels]
-                    term = jnp.where(flag > 0.0, term, 0.0)
-                if k == 0:
-                    acc_ref[i, r] = term
-                elif k == 1:
-                    acc_ref[i, r] = acc_ref[i, r] + term
-                else:
-                    y = acc_ref[i, r] + term + bias + h_ref[2 + i, r + 1].astype(F32)
-                    out_ref[i, r] = y.astype(BF16)
+
+    def convolve(i, k):
+        taps = [early_ref[t] if t < EARLY else late_ref[t - EARLY] for t in range(9 * k, 9 * k + 9)]
+        for r in range(2):
+            term = None
+            for dy in range(3):
+                for dx in range(3):
+                    d = jnp.dot(act_ref[i + k, r + dy, dx], taps[3 * dy + dx], preferred_element_type=F32)
+                    term = d if term is None else term + d
+            if k < 2:
+                flag = flags_ref[2 * (i + 2) + k : 2 * (i + 2) + k + 1, :channels]
+                term = jnp.where(flag > 0.0, term, 0.0)
+            if k == 0:
+                acc_ref[i, r] = term
+            elif k == 1:
+                acc_ref[i, r] = acc_ref[i, r] + term
+            else:
+                y = acc_ref[i, r] + term + bias + h_ref[2 + i, r + 1].astype(F32)
+                out_ref[i, r] = y.astype(BF16)
+                results.append(pltpu.make_async_copy(out_ref.at[i, r], out_hbm.at[i, r], out_sem.at[i, r]))
+                results[-1].start()
+
+    activate(0)
+    convolve(0, 0)
+    activate(1)
+    convolve(1, 0)
+    activate(2)
+    late.wait()
+    convolve(0, 1)
+    convolve(1, 1)
+    activate(3)
+    convolve(0, 2)
+    convolve(1, 2)
+    for copy in results:
+        copy.wait()
 
 
 def body(latents, frame_slot, lengths, w_in, bias_in, norm_gain, w_mid, bias_mid):
@@ -230,7 +237,7 @@
     tiles = lax.axis_size("tile")
     whole = jnp.concatenate([frame_slot, lengths])
     latents, whole = lax.optimization_barrier((latents, whole))
-    gathered = lax.all_gather(latents, "tm", axis=0, tiled=True)
+    gathered = lax.all_gather(latents, "tm", axis=0, tiled=True, axis_index_groups=[TIMES])
 
     def pick_body(*refs):
         pick_kernel(zc, frame_slot.shape[0], *refs)
@@ -241,6 +248,7 @@
         in_specs=[SMEM, VMEM],
         out_specs=[VMEM, VMEM],
         scratch_shapes=[
+            pltpu.SMEM(frame_slot.shape, jnp.int32),
             pltpu.VMEM((6,) + latents.shape[1:], F32),
         ],
         compiler_params=PARAMS,
@@ -249,7 +257,7 @@
     above = lax.ppermute(picked, "tile", [(i, i + 1) for i in range(tiles - 1)])
     below = lax.ppermute(picked, "tile", [(i + 1, i) for i in range(tiles - 1)])
     w_in = jnp.transpose(w_in, (1, 0, 2)).reshape(27 * zc, channels).astype(F32)
-    w_in = jnp.concatenate([w_in, jnp.broadcast_to(bias_in[None], (8, channels))], axis=0)
+    w_in = jnp.concatenate([w_in, jnp.broadcast_to(bias_in[None], (8, channels))], axis=0).T
     w_mid = jnp.transpose(w_mid, (1, 0, 2))
 
     def sums_body(*refs):
@@ -271,7 +279,7 @@
         compiler_params=PARAMS,
         name="sums",
     )(flags, above, picked, w_in)
-    sums = lax.all_to_all(sums, "tile", 0, 0)
+    sums = lax.all_to_all(sums, "tile", 0, 0, axis_index_groups=[TILES])
     hidden, early = pl.pallas_call(
         hidden_body,
         out_shape=[
@@ -297,12 +305,14 @@
         decode_body,
         out_shape=jax.ShapeDtypeStruct((2, rows, width, channels), BF16),
         in_specs=[VMEM, VMEM, VMEM, VMEM, HBM, VMEM, VMEM],
-        out_specs=VMEM,
+        out_specs=HBM,
         scratch_shapes=[
             pltpu.VMEM((4, 4, 3, width, channels), BF16),
             pltpu.VMEM((2, 2, width, channels), F32),
             pltpu.VMEM((27 - EARLY, channels, channels), BF16),
-            pltpu.SemaphoreType.DMA((2,)),
+            pltpu.VMEM((2, 2, width, channels), BF16),
+            pltpu.SemaphoreType.DMA,
+            pltpu.SemaphoreType.DMA((2, 2)),
         ],
         compiler_params=pltpu.CompilerParams(vmem_limit_bytes=52000 * 1024),
         name="decode",

time: 58.3 us -> 53.4 us (0.916); the launches traced: 58 us -> 52.5 us
  waiting for transfers between devices: 7.28 us -> 0.52 us
  starting transfers between devices: 17.4 us -> 20.6 us
  Pallas kernels: 9.44 us -> 8.14 us
  blocking collectives: 22 us -> 21.1 us
    all_to_all x1, waiting for transfers between devices: 7.27 us -> 0.52 us  [body(): sums = lax.all_to_all(sums, 'tile', 0, 0, axis_index_groups=[TILES])]
    all_to_all x1, starting transfers between devices: 14.1 us -> 17.5 us  [body(): sums = lax.all_to_all(sums, 'tile', 0, 0, axis_index_groups=[TILES])]
    all_gather x1, blocking collectives: 22 us -> 21.1 us  [body(): lax.all_gather(latents, 'tm', axis=0, tiled=True, axis_index_groups=[TIMES])]
    pallas_call x1, Pallas kernels: 4.84 us -> 4.19 us  [body(): pl.pallas_call(decode_body, out_shape=jax.ShapeDtypeStruct((2, rows, widt...]
  transfers between devices with their start and end apart: 3 -> 3, of which waited for: 1 -> 1; matrix products, arithmetic and copies ran while one was open for 2% -> 3% of each run, Pallas kernels for 6% -> 6%
where the time goes in v4:
time: 53.4 us; the launch traced here: 52.5 us
  blocking collectives  21.1 us (40%)
  starting transfers between devices  20.6 us (39%)
  Pallas kernels  8.14 us (15%)
  other arithmetic  1.83 us (3%)
    all_gather x1, blocking collectives, body(): lax.all_gather(latents, 'tm', axis=0, tiled=True, axis_index_groups=[TIMES])  21.1 us
    all_to_all x1, starting transfers between devices, body(): sums = lax.all_to_all(sums, 'tile', 0, 0, axis_index_groups=[TILES])  17.5 us
    pallas_call x1, Pallas kernels, body(): pl.pallas_call(decode_body, out_shape=jax.ShapeDtypeStruct((2, rows, widt...  4.19 us
    ppermute x1, starting transfers between devices, body(): above = lax.ppermute(picked, 'tile', [(i, i + 1) for i in range(tiles - 1)])  1.75 us
    pallas_call x1, Pallas kernels, body(): pl.pallas_call(sums_body, out_shape=jax.ShapeDtypeStruct((tiles, 2, 128),...  1.67 us
    pallas_call x1, Pallas kernels, body(): pl.pallas_call(hidden_body, out_shape=[jax.ShapeDtypeStruct((4, 4, width,...  1.32 us
    ppermute x1, starting transfers between devices, body(): below = lax.ppermute(picked, 'tile', [(i + 1, i) for i in range(tiles - 1)])  1.29 us
  transfers between devices with their start and end apart: 3, of which 1 were waited for; matrix products, arithmetic and copies ran while one was open for 3% of the time, Pallas kernels for 6%

profile of v4, /device:TPU:1, one launch (start us, length us, event | category | flops | bytes accessed | tf_op | source)
XLA Modules:
  0.0 52.5 jit_solution(11552338778471243075)
XLA Ops:
  0.0 0.0 copy-start.2
  0.0 0.8 %pad_add_fusion.refs_0_ = s32[36]{0:T(128)S(1)} fusion(s32[4]{0:T(128)} %param.10, s32[32]{0:T(128)} %param.9), kind=kLoop, calls=%fused_computation.1 | loop fusion | flops 36 | bytes 288 | tf_op jit(solution)/shard_map/concatenate | solution.py:238
  0.8 21.1 %all_gather.3.refs_1_ = bf16[32,2,2560]{2,1,0:T(2,128)(2,1)S(1)} all-gather(bf16[2,2,2560]{2,1,0:T(2,128)(2,1)} %param.8), channel_id=1, replica_groups={{480,448,416,384,352,320,288,256,224,192,160,128,96,64,32,0},{481,449,4..., dimensions={0}, use_global_device_ids=true | all-gather | bytes 348160 | tf_op jit(solution)/shard_map/all_gather | solution.py:240
  21.8 1.0 %pick.1 = (bf16[6,2,16,256]{3,2,1,0:T(8,128)(2,1)S(1)}, f32[8,256]{1,0:T(8,128)S(1)}) custom-call(s32[36]{0:T(128)S(1)} %pad_add_fusion.refs_0_, bf16[32,2,2560]{2,1,0:T(2,128)(2,1)S(1)} %all_gather.3.refs_1_), custom_call_target="tpu_custom_call" | custom-call | tf_op jit(solution)/shard_map/pick/pallas_call | solution.py:245
  22.8 1.7 %collective-permute-start = (bf16[6,2,16,256]{3,2,1,0:T(8,128)(2,1)S(1)}, bf16[6,2,16,256]{3,2,1,0:T(8,128)(2,1)S(1)}, u32[]{:S(2)}, u32[]{:S(2)}) collective-permute-start(bf16[6,2,16,256]{3,2,1,0:T(8,128)(2,1)S(1)} %get-tuple-element.14.refs_2_), channel_id=1, source_target_pairs={{0,1},{1,2},{2,3},{3,4},{4,5},{5,6},{6,7},{7,8},{8,9},{9,10},{10,1... | collective-permute-start | bytes 294920 | tf_op jit(solution)/shard_map/ppermute | solution.py:257
  24.5 1.3 %collective-permute-start.1 = (bf16[6,2,16,256]{3,2,1,0:T(8,128)(2,1)S(1)}, bf16[6,2,16,256]{3,2,1,0:T(8,128)(2,1)S(1)}, u32[]{:S(2)}, u32[]{:S(2)}) collective-permute-start(bf16[6,2,16,256]{3,2,1,0:T(8,128)(2,1)S(1)} %get-tuple-element.14.refs_2_), channel_id=1, source_target_pairs={{1,0},{2,1},{3,2},{4,3},{5,4},{6,5},{7,6},{8,7},{9,8},{10,9},{11,1... | collective-permute-start | bytes 294920 | tf_op jit(solution)/shard_map/ppermute | solution.py:258
  25.8 1.0 %convert_element_type.13 = f32[16,27,192]{2,0,1:T(8,128)S(1)} convert(bf16[16,27,192]{2,0,1:T(8,128)(2,1)} %param.11) | non-fusion elementwise | flops 82944 | bytes 497664 | tf_op jit(solution)/shard_map/convert_element_type | solution.py:259
  26.8 0.2 copy.11
  27.0 0.0 copy-done.2
  27.0 0.1 broadcast_in_dim.12
  27.1 0.1 maximum_bitcast_fusion.refs_3_.refs_4_
  27.2 0.0 collective-permute-done.refs_1_
  27.2 1.7 %sums.1 = f32[32,2,128]{2,1,0:T(2,128)} custom-call(f32[8,256]{1,0:T(8,128)S(1)} %get-tuple-element.13.refs_0_, bf16[6,2,16,256]{3,2,1,0:T(8,128)(2,1)S(1)} %collective-permute-done.refs_1_, bf16[6,2,16,256]{3,2,1,0:T(8,128)(2,1)S(1)} %get-tuple-element.14.refs_2_, f32[192,440]{1,0:T(8,128)S(1)} %maximum_bitcast_fusion.refs_3_.refs_4_), custom_call_target="tpu_custom_call" | custom-call | tf_op jit(solution)/shard_map/sums/pallas_call | solution.py:269
  28.9 17.5 %all-to-all-start = ((f32[32,2,128]{2,1,0:T(2,128)}), f32[32,2,128]{2,1,0:T(2,128)S(1)}, u32[]{:S(2)}, u32[]{:S(2)}) async-start(f32[32,2,128]{2,1,0:T(2,128)} %sums.1), calls=%async_computation | async-start | bytes 65536 | tf_op jit(solution)/shard_map/all_to_all | solution.py:282
  46.4 0.0 collective-permute-done.1.refs_3_
  46.4 0.0 copy-start
  46.5 0.0 copy-start.1
  46.5 1.3 %hidden.1 = (bf16[4,4,160,192]{3,2,1,0:T(8,128)(2,1)S(1)}, bf16[13,192,192]{2,1,0:T(8,128)(2,1)S(1)}) custom-call(f32[8,256]{1,0:T(8,128)S(1)} %get-tuple-element.13.refs_0_, bf16[6,2,16,256]{3,2,1,0:T(8,128)(2,1)S(1)} %collective-permute-done.refs_1_, bf16[6,2,16,256]{3,2,1,0:T(8,128)(2,1)S(1)} %get-tuple-element.14.refs_2_, ...), custom_call_target="tpu_custom_call" | custom-call | flops 4000000000 | bytes 2000000 | tf_op jit(solution)/shard_map/hidden/pallas_call | solution.py:283
  47.8 0.5 all-to-all-done.refs_1_
  48.3 0.0 copy-done
  48.3 0.0 copy-done.1
  48.3 4.2 %decode.1 = bf16[2,2,160,192]{3,2,1,0:T(8,128)(2,1)} custom-call(f32[8,256]{1,0:T(8,128)S(1)} %get-tuple-element.13.refs_0_, f32[32,2,128]{2,1,0:T(2,128)S(1)} %all-to-all-done.refs_1_, bf16[4,4,160,192]{3,2,1,0:T(8,128)(2,1)S(1)} %get-tuple-element.15.refs_2_, bf16[13,192,192]{2,1,0:T(8,128)(2,1)S(1)} %get-tuple-element.16.refs_3_, ...), custom_call_target="tpu_custom_call" | custom-call | tf_op jit(solution)/shard_map/decode/pallas_call | solution.py:304
Async XLA Ops:
  0.0 27.0 %copy-start.2 = (f32[192]{0:T(256)S(1)}, f32[192]{0:T(256)}, u32[]{:S(2)}) copy-start(f32[192]{0:T(256)} %param.12) | copy-start | bytes 2308
  22.8 4.4 %collective-permute-start = (bf16[6,2,16,256]{3,2,1,0:T(8,128)(2,1)S(1)}, bf16[6,2,16,256]{3,2,1,0:T(8,128)(2,1)S(1)}, u32[]{:S(2)}, u32[]{:S(2)}) collective-permute-start(bf16[6,2,16,256]{3,2,1,0:T(8,128)(2,1)S(1)} %get-tuple-element.14.refs_2_), channel_id=1, source_target_pairs={{0,1},{1,2},{2,3},{3,4},{4,5},{5,6},{6,7},{7,8},{8,9},{9,10},{10,1... | collective-permute-start | bytes 294920 | tf_op jit(solution)/shard_map/ppermute | solution.py:257
  24.5 21.9 %collective-permute-start.1 = (bf16[6,2,16,256]{3,2,1,0:T(8,128)(2,1)S(1)}, bf16[6,2,16,256]{3,2,1,0:T(8,128)(2,1)S(1)}, u32[]{:S(2)}, u32[]{:S(2)}) collective-permute-start(bf16[6,2,16,256]{3,2,1,0:T(8,128)(2,1)S(1)} %get-tuple-element.14.refs_2_), channel_id=1, source_target_pairs={{1,0},{2,1},{3,2},{4,3},{5,4},{6,5},{7,6},{8,7},{9,8},{10,9},{11,1... | collective-permute-start | bytes 294920 | tf_op jit(solution)/shard_map/ppermute | solution.py:258
  28.9 19.4 %all-to-all-start = ((f32[32,2,128]{2,1,0:T(2,128)}), f32[32,2,128]{2,1,0:T(2,128)S(1)}, u32[]{:S(2)}, u32[]{:S(2)}) async-start(f32[32,2,128]{2,1,0:T(2,128)} %sums.1), calls=%async_computation | async-start | bytes 65536 | tf_op jit(solution)/shard_map/all_to_all | solution.py:282
  46.4 1.9 %copy-start = (f32[192]{0:T(256)S(1)}, f32[192]{0:T(256)}, u32[]{:S(2)}) copy-start(f32[192]{0:T(256)} %param.13) | copy-start | bytes 2308
  46.5 1.9 %copy-start.1 = (f32[192]{0:T(256)S(1)}, f32[192]{0:T(256)}, u32[]{:S(2)}) copy-start(f32[192]{0:T(256)} %param.15) | copy-start | bytes 2308

commit v5 on v4

--- a/solution.py
+++ b/solution.py
@@ -8,7 +8,7 @@
 GROUPS = 32
 LANES = 256
 EARLY = 13
-TIMES = list(range(15, -1, -1))
+CHIPS = [5, 6, 7, 4, 3, 2, 1, 0]
 TILES = [8 * x + z for z in (4, 5, 6, 7, 3, 2, 1, 0) for x in (2, 3, 1, 0)]
 VMEM = pl.BlockSpec(memory_space=pltpu.VMEM)
 SMEM = pl.BlockSpec(memory_space=pltpu.SMEM)
@@ -31,7 +31,7 @@
 def pick_kernel(zc, frames, whole_ref, gathered_ref, picked_ref, flags_ref, where_ref, raw_ref):
     first = 2 * lax.axis_index("tm")
     for p in range(frames):
-        where_ref[whole_ref[p]] = 2 * TIMES.index(p // 2) + p % 2
+        where_ref[whole_ref[p]] = 16 * (p // 2 % 2) + 2 * CHIPS.index(p // 4) + p % 2
     for j in range(6):
         t = first - 4 + j
         raw = gathered_ref[where_ref[jnp.maximum(t, 0)]].astype(F32)
@@ -236,8 +236,10 @@
     width = latents.shape[2] // zc
     tiles = lax.axis_size("tile")
     whole = jnp.concatenate([frame_slot, lengths])
-    latents, whole = lax.optimization_barrier((latents, whole))
-    gathered = lax.all_gather(latents, "tm", axis=0, tiled=True, axis_index_groups=[TIMES])
+    cores = [[2 * y + c for y in CHIPS] for c in range(2)]
+    column = lax.all_to_all(jnp.broadcast_to(latents[None], (8,) + latents.shape), "tm", 0, 0, axis_index_groups=cores)
+    gathered = lax.all_gather(column, "tm", axis=0, axis_index_groups=[[2 * y, 2 * y + 1] for y in range(8)])
+    gathered = gathered.reshape((32,) + latents.shape[1:])
 
     def pick_body(*refs):
         pick_kernel(zc, frame_slot.shape[0], *refs)

time: 53.4 us -> 51.9 us (0.972)
  blocking collectives: 21.1 us -> 6.81 us
  starting transfers between devices: 20.6 us -> 29.6 us
  waiting for transfers between devices: 0.52 us -> 3.41 us
  local copies, waits for them, and re-layouts: 0.28 us -> 1.79 us
  other arithmetic: 1.83 us -> 1.15 us
    all_gather x1, blocking collectives: 21.1 us -> 6.81 us  [body(): lax.all_gather(column, 'tm', axis=0, axis_index_groups=[[2 * y, 2 * y + 1...]
    all_to_all x0 -> x1, starting transfers between devices: none -> 9.05 us  [body(): lax.all_to_all(jnp.broadcast_to(latents[None], (8,) + latents.shape), 'tm...]
    all_to_all x0 -> x1, waiting for transfers between devices: none -> 2.6 us  [body(): lax.all_to_all(jnp.broadcast_to(latents[None], (8,) + latents.shape), 'tm...]
    broadcast_in_dim x0 -> x1, local copies, waits for them, and re-layouts: none -> 1.51 us  [body(): jnp.broadcast_to(latents[None], (8,) + latents.shape)]
    concatenate x1, other arithmetic: 0.76 us -> 0.08 us  [body(): whole = jnp.concatenate([frame_slot, lengths])]
  transfers between devices with their start and end apart: 3 -> 4, of which waited for: 1 -> 3; matrix products, arithmetic and copies ran while one was open for 3% -> 3% of each run, Pallas kernels for 6% -> 6%
where the time goes in v5:
time: 51.9 us; the launch traced here: 51 us
  starting transfers between devices  29.6 us (57%)
  Pallas kernels  8.13 us (16%)
  blocking collectives  6.81 us (13%)
  waiting for transfers between devices  3.41 us (7%)
  local copies, waits for them, and re-layouts  1.79 us (3%)
  other arithmetic  1.15 us (2%)
    all_to_all x1, starting transfers between devices, body(): sums = lax.all_to_all(sums, 'tile', 0, 0, axis_index_groups=[TILES])  18 us
    all_to_all x1, starting transfers between devices, body(): lax.all_to_all(jnp.broadcast_to(latents[None], (8,) + latents.shape), 'tm...  9.05 us
    all_gather x1, blocking collectives, body(): lax.all_gather(column, 'tm', axis=0, axis_index_groups=[[2 * y, 2 * y + 1...  6.81 us
    pallas_call x1, Pallas kernels, body(): pl.pallas_call(decode_body, out_shape=jax.ShapeDtypeStruct((2, rows, widt...  4.19 us
    all_to_all x1, waiting for transfers between devices, body(): lax.all_to_all(jnp.broadcast_to(latents[None], (8,) + latents.shape), 'tm...  2.6 us
    pallas_call x1, Pallas kernels, body(): pl.pallas_call(sums_body, out_shape=jax.ShapeDtypeStruct((tiles, 2, 128),...  1.66 us
    broadcast_in_dim x1, local copies, waits for them, and re-layouts, body(): jnp.broadcast_to(latents[None], (8,) + latents.shape)  1.51 us
    pallas_call x1, Pallas kernels, body(): pl.pallas_call(hidden_body, out_shape=[jax.ShapeDtypeStruct((4, 4, width,...  1.32 us
  transfers between devices with their start and end apart: 4, of which 3 were waited for; matrix products, arithmetic and copies ran while one was open for 3% of the time, Pallas kernels for 6%

profile of v5, /device:TPU:1, one launch (start us, length us, event | category | flops | bytes accessed | tf_op | source)
XLA Modules:
  0.0 51.0 jit_solution(14425527435914575510)
XLA Ops:
  0.0 0.0 copy-start.3
  0.0 0.0 copy-start.4
  0.0 1.5 %broadcast_in_dim.8 = bf16[8,2,2,2560]{3,2,1,0:T(2,128)(2,1)} broadcast(bf16[2,2,2560]{2,1,0:T(2,128)(2,1)} %param.8), dimensions={1,2,3} | broadcast | bytes 184320 | tf_op jit(solution)/shard_map/broadcast_in_dim | solution.py:240
  1.5 0.0 copy-start.2
  1.5 9.0 %all-to-all-start = ((bf16[8,2,2,2560]{3,2,1,0:T(2,128)(2,1)}), bf16[8,2,2,2560]{3,2,1,0:T(2,128)(2,1)S(1)}, u32[]{:S(2)}, u32[]{:S(2)}) async-start(bf16[8,2,2,2560]{3,2,1,0:T(2,128)(2,1)} %broadcast_in_dim.8), calls=%async_computation | async-start | bytes 327680 | tf_op jit(solution)/shard_map/all_to_all | solution.py:240
  10.6 1.0 %convert_element_type.13 = f32[16,27,192]{2,0,1:T(8,128)S(1)} convert(bf16[16,27,192]{2,0,1:T(8,128)(2,1)} %param.11) | non-fusion elementwise | flops 82944 | bytes 497664 | tf_op jit(solution)/shard_map/convert_element_type | solution.py:261
  11.5 0.2 copy.11
  11.7 0.0 copy-done.3
  11.7 0.0 copy-done.4
  11.7 0.1 pad_add_fusion.refs_0_
  11.8 2.6 %all-to-all-done = bf16[8,2,2,2560]{3,2,1,0:T(2,128)(2,1)S(1)} async-done(((bf16[8,2,2,2560]{3,2,1,0:T(2,128)(2,1)}), bf16[8,2,2,2560]{3,2,1,0:T(2,128)(2,1)S(1)}, u32[]{:S(2)}, u32[]{:S(2)}) %all-to-all-start) | async-done | bytes 163872 | tf_op jit(solution)/shard_map/all_to_all | solution.py:240
  14.4 6.8 %all-gather = bf16[16,2,2,2560]{3,2,1,0:T(2,128)(2,1)S(1)} all-gather(bf16[8,2,2,2560]{3,2,1,0:T(2,128)(2,1)S(1)} %all-to-all-done), channel_id=2, replica_groups={{0,32},{64,96},{128,160},{192,224},{256,288},{320,352},{384,416},{448,4..., dimensions={0}, use_global_device_ids=true | all-gather | bytes 491520 | tf_op jit(solution)/shard_map/all_gather | solution.py:241
  21.2 1.0 %pick.1 = (bf16[6,2,16,256]{3,2,1,0:T(8,128)(2,1)S(1)}, f32[8,256]{1,0:T(8,128)S(1)}) custom-call(s32[36]{0:T(128)S(1)} %pad_add_fusion.refs_0_, bf16[32,2,2560]{2,1,0:T(2,128)(2,1)S(1)} %bitcast.9), custom_call_target="tpu_custom_call" | custom-call | tf_op jit(solution)/shard_map/pick/pallas_call | solution.py:247
  22.2 1.3 %collective-permute-start = (bf16[6,2,16,256]{3,2,1,0:T(8,128)(2,1)S(1)}, bf16[6,2,16,256]{3,2,1,0:T(8,128)(2,1)S(1)}, u32[]{:S(2)}, u32[]{:S(2)}) collective-permute-start(bf16[6,2,16,256]{3,2,1,0:T(8,128)(2,1)S(1)} %get-tuple-element.10.refs_2_), channel_id=1, source_target_pairs={{0,1},{1,2},{2,3},{3,4},{4,5},{5,6},{6,7},{7,8},{8,9},{9,10},{10,1... | collective-permute-start | bytes 294920 | tf_op jit(solution)/shard_map/ppermute | solution.py:259
  23.5 1.3 %collective-permute-start.1 = (bf16[6,2,16,256]{3,2,1,0:T(8,128)(2,1)S(1)}, bf16[6,2,16,256]{3,2,1,0:T(8,128)(2,1)S(1)}, u32[]{:S(2)}, u32[]{:S(2)}) collective-permute-start(bf16[6,2,16,256]{3,2,1,0:T(8,128)(2,1)S(1)} %get-tuple-element.10.refs_2_), channel_id=1, source_target_pairs={{1,0},{2,1},{3,2},{4,3},{5,4},{6,5},{7,6},{8,7},{9,8},{10,9},{11,1... | collective-permute-start | bytes 294920 | tf_op jit(solution)/shard_map/ppermute | solution.py:260
  24.8 0.0 copy-done.2
  24.8 0.1 broadcast_in_dim.9
  24.9 0.1 maximum_bitcast_fusion.refs_3_.refs_4_
  25.0 0.3 collective-permute-done.refs_1_
  25.3 1.7 %sums.1 = f32[32,2,128]{2,1,0:T(2,128)} custom-call(f32[8,256]{1,0:T(8,128)S(1)} %get-tuple-element.9.refs_0_, bf16[6,2,16,256]{3,2,1,0:T(8,128)(2,1)S(1)} %collective-permute-done.refs_1_, bf16[6,2,16,256]{3,2,1,0:T(8,128)(2,1)S(1)} %get-tuple-element.10.refs_2_, f32[192,440]{1,0:T(8,128)S(1)} %maximum_bitcast_fusion.refs_3_.refs_4_), custom_call_target="tpu_custom_call" | custom-call | tf_op jit(solution)/shard_map/sums/pallas_call | solution.py:271
  27.0 18.0 %all-to-all-start.1 = ((f32[32,2,128]{2,1,0:T(2,128)}), f32[32,2,128]{2,1,0:T(2,128)S(1)}, u32[]{:S(2)}, u32[]{:S(2)}) async-start(f32[32,2,128]{2,1,0:T(2,128)} %sums.1), calls=%async_computation.1 | async-start | bytes 65536 | tf_op jit(solution)/shard_map/all_to_all | solution.py:284
  45.0 0.0 collective-permute-done.1.refs_3_
  45.0 0.0 copy-start
  45.0 0.0 copy-start.1
  45.0 1.3 %hidden.1 = (bf16[4,4,160,192]{3,2,1,0:T(8,128)(2,1)S(1)}, bf16[13,192,192]{2,1,0:T(8,128)(2,1)S(1)}) custom-call(f32[8,256]{1,0:T(8,128)S(1)} %get-tuple-element.9.refs_0_, bf16[6,2,16,256]{3,2,1,0:T(8,128)(2,1)S(1)} %collective-permute-done.refs_1_, bf16[6,2,16,256]{3,2,1,0:T(8,128)(2,1)S(1)} %get-tuple-element.10.refs_2_, ...), custom_call_target="tpu_custom_call" | custom-call | flops 4000000000 | bytes 2000000 | tf_op jit(solution)/shard_map/hidden/pallas_call | solution.py:285
  46.3 0.5 %all-to-all-done.1.refs_1_ = f32[32,2,128]{2,1,0:T(2,128)S(1)} async-done(((f32[32,2,128]{2,1,0:T(2,128)}), f32[32,2,128]{2,1,0:T(2,128)S(1)}, u32[]{:S(2)}, u32[]{:S(2)}) %all-to-all-start.1) | async-done | bytes 32800 | tf_op jit(solution)/shard_map/all_to_all | solution.py:284
  46.8 0.0 copy-done
  46.8 0.0 copy-done.1
  46.8 4.2 %decode.1 = bf16[2,2,160,192]{3,2,1,0:T(8,128)(2,1)} custom-call(f32[8,256]{1,0:T(8,128)S(1)} %get-tuple-element.9.refs_0_, f32[32,2,128]{2,1,0:T(2,128)S(1)} %all-to-all-done.1.refs_1_, bf16[4,4,160,192]{3,2,1,0:T(8,128)(2,1)S(1)} %get-tuple-element.11.refs_2_, bf16[13,192,192]{2,1,0:T(8,128)(2,1)S(1)} %get-tuple-element.12.refs_3_, ...), custom_call_target="tpu_custom_call" | custom-call | tf_op jit(solution)/shard_map/decode/pallas_call | solution.py:306
Async XLA Ops:
  0.0 11.7 %copy-start.3 = (s32[4]{0:T(128)S(1)}, s32[4]{0:T(128)}, u32[]{:S(2)}) copy-start(s32[4]{0:T(128)} %param.10) | copy-start | bytes 52
  0.0 11.7 %copy-start.4 = (s32[32]{0:T(128)S(1)}, s32[32]{0:T(128)}, u32[]{:S(2)}) copy-start(s32[32]{0:T(128)} %param.9) | copy-start | bytes 388
  1.5 23.3 %copy-start.2 = (f32[192]{0:T(256)S(1)}, f32[192]{0:T(256)}, u32[]{:S(2)}) copy-start(f32[192]{0:T(256)} %param.12) | copy-start | bytes 2308
  1.5 12.9 %all-to-all-start = ((bf16[8,2,2,2560]{3,2,1,0:T(2,128)(2,1)}), bf16[8,2,2,2560]{3,2,1,0:T(2,128)(2,1)S(1)}, u32[]{:S(2)}, u32[]{:S(2)}) async-start(bf16[8,2,2,2560]{3,2,1,0:T(2,128)(2,1)} %broadcast_in_dim.8), calls=%async_computation | async-start | bytes 327680 | tf_op jit(solution)/shard_map/all_to_all | solution.py:240
  22.2 3.1 %collective-permute-start = (bf16[6,2,16,256]{3,2,1,0:T(8,128)(2,1)S(1)}, bf16[6,2,16,256]{3,2,1,0:T(8,128)(2,1)S(1)}, u32[]{:S(2)}, u32[]{:S(2)}) collective-permute-start(bf16[6,2,16,256]{3,2,1,0:T(8,128)(2,1)S(1)} %get-tuple-element.10.refs_2_), channel_id=1, source_target_pairs={{0,1},{1,2},{2,3},{3,4},{4,5},{5,6},{6,7},{7,8},{8,9},{9,10},{10,1... | collective-permute-start | bytes 294920 | tf_op jit(solution)/shard_map/ppermute | solution.py:259
  23.5 21.5 %collective-permute-start.1 = (bf16[6,2,16,256]{3,2,1,0:T(8,128)(2,1)S(1)}, bf16[6,2,16,256]{3,2,1,0:T(8,128)(2,1)S(1)}, u32[]{:S(2)}, u32[]{:S(2)}) collective-permute-start(bf16[6,2,16,256]{3,2,1,0:T(8,128)(2,1)S(1)} %get-tuple-element.10.refs_2_), channel_id=1, source_target_pairs={{1,0},{2,1},{3,2},{4,3},{5,4},{6,5},{7,6},{8,7},{9,8},{10,9},{11,1... | collective-permute-start | bytes 294920 | tf_op jit(solution)/shard_map/ppermute | solution.py:260
  27.0 19.9 %all-to-all-start.1 = ((f32[32,2,128]{2,1,0:T(2,128)}), f32[32,2,128]{2,1,0:T(2,128)S(1)}, u32[]{:S(2)}, u32[]{:S(2)}) async-start(f32[32,2,128]{2,1,0:T(2,128)} %sums.1), calls=%async_computation.1 | async-start | bytes 65536 | tf_op jit(solution)/shard_map/all_to_all | solution.py:284
  45.0 1.9 %copy-start = (f32[192]{0:T(256)S(1)}, f32[192]{0:T(256)}, u32[]{:S(2)}) copy-start(f32[192]{0:T(256)} %param.13) | copy-start | bytes 2308
  45.0 1.9 %copy-start.1 = (f32[192]{0:T(256)S(1)}, f32[192]{0:T(256)}, u32[]{:S(2)}) copy-start(f32[192]{0:T(256)} %param.15) | copy-start | bytes 2308

commit v6 on v5

--- a/solution.py
+++ b/solution.py
@@ -7,7 +7,7 @@
 
 GROUPS = 32
 LANES = 256
-EARLY = 13
+EARLY = 16
 CHIPS = [5, 6, 7, 4, 3, 2, 1, 0]
 TILES = [8 * x + z for z in (4, 5, 6, 7, 3, 2, 1, 0) for x in (2, 3, 1, 0)]
 VMEM = pl.BlockSpec(memory_space=pltpu.VMEM)
@@ -84,7 +84,7 @@
 
 def frame_weights(w_ref, flags_ref):
     taps = w_ref.shape[1] - 8
-    whole = w_ref[:, :taps].astype(BF16)
+    whole = w_ref[:, :taps]
     lane = lax.broadcasted_iota(jnp.int32, (1, taps), 1)
     result = []
     for j in range(4):
@@ -92,7 +92,8 @@
         u1 = flags_ref[2 * j + 1 : 2 * j + 2, 0:1]
         keep = jnp.where(lane < taps // 3, u0, jnp.where(lane < 2 * taps // 3, u1, 1.0)).astype(BF16)
         result.append(whole * keep)
-    return result, w_ref[:, taps : taps + 1]
+    bias = w_ref[:, taps:].astype(F32)
+    return result, bias[:, 0:1] + bias[:, 1:2] + bias[:, 2:3]
 
 
 def hidden_t(weights, bias, xs_ref, j, r):
@@ -258,8 +259,11 @@
     )(whole, gathered)
     above = lax.ppermute(picked, "tile", [(i, i + 1) for i in range(tiles - 1)])
     below = lax.ppermute(picked, "tile", [(i + 1, i) for i in range(tiles - 1)])
-    w_in = jnp.transpose(w_in, (1, 0, 2)).reshape(27 * zc, channels).astype(F32)
-    w_in = jnp.concatenate([w_in, jnp.broadcast_to(bias_in[None], (8, channels))], axis=0).T
+    w_in = jnp.transpose(w_in, (1, 0, 2)).reshape(27 * zc, channels)
+    high = lax.reduce_precision(bias_in, 8, 7)
+    middle = lax.reduce_precision(bias_in - high, 8, 7)
+    parts = jnp.stack([high, middle, bias_in - high - middle] + [jnp.zeros_like(bias_in)] * 5)
+    w_in = jnp.concatenate([w_in, parts.astype(BF16)], axis=0).T
     w_mid = jnp.transpose(w_mid, (1, 0, 2))
 
     def sums_body(*refs):

time: 51.9 us -> 52 us (level)
    convert_element_type x1 -> x0, other arithmetic: 0.97 us -> none  [body(): w_in = jnp.transpose(w_in, (1, 0, 2)).reshape(27 * zc, channels).astype(F32)]
    another operation x0 -> x1, other arithmetic: none -> 0.69 us
    concatenate x1, other arithmetic: 0.08 us -> 0.75 us  [body(): whole = jnp.concatenate([frame_slot, lengths])]
    all_to_all x1, waiting for transfers between devices: 2.6 us -> 3.12 us  [body(): lax.all_to_all(jnp.broadcast_to(latents[None], (8,) + latents.shape), 'tm...]
  transfers between devices with their start and end apart: 4 -> 4, of which waited for: 3 -> 2; matrix products, arithmetic and copies ran while one was open for 3% -> 4% of each run, Pallas kernels for 6% -> 6%
where the time goes in v6:
time: 52 us; the launch traced here: 51.4 us
  starting transfers between devices  29.1 us (56%)
  Pallas kernels  8.3 us (16%)
  blocking collectives  6.81 us (13%)
  waiting for transfers between devices  3.54 us (7%)
  local copies, waits for them, and re-layouts  2.1 us (4%)
  other arithmetic  1.43 us (3%)
    all_to_all x1, starting transfers between devices, body(): sums = lax.all_to_all(sums, 'tile', 0, 0, axis_index_groups=[TILES])  17.6 us
    all_to_all x1, starting transfers between devices, body(): lax.all_to_all(jnp.broadcast_to(latents[None], (8,) + latents.shape), 'tm...  8.91 us
    all_gather x1, blocking collectives, body(): lax.all_gather(column, 'tm', axis=0, axis_index_groups=[[2 * y, 2 * y + 1...  6.81 us
    pallas_call x1, Pallas kernels, body(): pl.pallas_call(decode_body, out_shape=jax.ShapeDtypeStruct((2, rows, widt...  4.2 us
    all_to_all x1, waiting for transfers between devices, body(): lax.all_to_all(jnp.broadcast_to(latents[None], (8,) + latents.shape), 'tm...  3.12 us
    pallas_call x1, Pallas kernels, body(): pl.pallas_call(sums_body, out_shape=jax.ShapeDtypeStruct((tiles, 2, 128),...  1.72 us
    broadcast_in_dim x1, local copies, waits for them, and re-layouts, body(): jnp.broadcast_to(latents[None], (8,) + latents.shape)  1.52 us
    pallas_call x1, Pallas kernels, body(): pl.pallas_call(hidden_body, out_shape=[jax.ShapeDtypeStruct((4, 4, width,...  1.43 us
  transfers between devices with their start and end apart: 4, of which 2 were waited for; matrix products, arithmetic and copies ran while one was open for 4% of the time, Pallas kernels for 6%

profile of v6, /device:TPU:1, one launch (start us, length us, event | category | flops | bytes accessed | tf_op | source)
XLA Modules:
  0.0 51.4 jit_solution(16468978424129627329)
XLA Ops:
  0.0 0.0 copy-start.2
  0.0 1.5 %broadcast_in_dim.12 = bf16[8,2,2,2560]{3,2,1,0:T(2,128)(2,1)} broadcast(bf16[2,2,2560]{2,1,0:T(2,128)(2,1)} %param.8), dimensions={1,2,3} | broadcast | bytes 184320 | tf_op jit(solution)/shard_map/broadcast_in_dim | solution.py:241
  1.5 8.9 %all-to-all-start = ((bf16[8,2,2,2560]{3,2,1,0:T(2,128)(2,1)}), bf16[8,2,2,2560]{3,2,1,0:T(2,128)(2,1)S(1)}, u32[]{:S(2)}, u32[]{:S(2)}) async-start(bf16[8,2,2,2560]{3,2,1,0:T(2,128)(2,1)} %broadcast_in_dim.12), calls=%async_computation | async-start | bytes 327680 | tf_op jit(solution)/shard_map/all_to_all | solution.py:241
  10.4 0.7 %pad_add_fusion.refs_0_ = s32[36]{0:T(128)S(1)} fusion(s32[4]{0:T(128)} %param.10, s32[32]{0:T(128)} %param.9), kind=kLoop, calls=%fused_computation.5 | loop fusion | flops 36 | bytes 288 | tf_op jit(solution)/shard_map/concatenate | solution.py:239
  11.2 3.1 %all-to-all-done = bf16[8,2,2,2560]{3,2,1,0:T(2,128)(2,1)S(1)} async-done(((bf16[8,2,2,2560]{3,2,1,0:T(2,128)(2,1)}), bf16[8,2,2,2560]{3,2,1,0:T(2,128)(2,1)S(1)}, u32[]{:S(2)}, u32[]{:S(2)}) %all-to-all-start) | async-done | bytes 163872 | tf_op jit(solution)/shard_map/all_to_all | solution.py:241
  14.3 6.8 %all-gather = bf16[16,2,2,2560]{3,2,1,0:T(2,128)(2,1)S(1)} all-gather(bf16[8,2,2,2560]{3,2,1,0:T(2,128)(2,1)S(1)} %all-to-all-done), channel_id=2, replica_groups={{0,32},{64,96},{128,160},{192,224},{256,288},{320,352},{384,416},{448,4..., dimensions={0}, use_global_device_ids=true | all-gather | bytes 491520 | tf_op jit(solution)/shard_map/all_gather | solution.py:242
  21.1 1.0 %pick.1 = (bf16[6,2,16,256]{3,2,1,0:T(8,128)(2,1)S(1)}, f32[8,256]{1,0:T(8,128)S(1)}) custom-call(s32[36]{0:T(128)S(1)} %pad_add_fusion.refs_0_, bf16[32,2,2560]{2,1,0:T(2,128)(2,1)S(1)} %bitcast.8), custom_call_target="tpu_custom_call" | custom-call | tf_op jit(solution)/shard_map/pick/pallas_call | solution.py:248
  22.1 1.3 %collective-permute-start = (bf16[6,2,16,256]{3,2,1,0:T(8,128)(2,1)S(1)}, bf16[6,2,16,256]{3,2,1,0:T(8,128)(2,1)S(1)}, u32[]{:S(2)}, u32[]{:S(2)}) collective-permute-start(bf16[6,2,16,256]{3,2,1,0:T(8,128)(2,1)S(1)} %get-tuple-element.10.refs_2_), channel_id=1, source_target_pairs={{0,1},{1,2},{2,3},{3,4},{4,5},{5,6},{6,7},{7,8},{8,9},{9,10},{10,1... | collective-permute-start | bytes 294920 | tf_op jit(solution)/shard_map/ppermute | solution.py:260
  23.4 1.3 %collective-permute-start.1 = (bf16[6,2,16,256]{3,2,1,0:T(8,128)(2,1)S(1)}, bf16[6,2,16,256]{3,2,1,0:T(8,128)(2,1)S(1)}, u32[]{:S(2)}, u32[]{:S(2)}) collective-permute-start(bf16[6,2,16,256]{3,2,1,0:T(8,128)(2,1)S(1)} %get-tuple-element.10.refs_2_), channel_id=1, source_target_pairs={{1,0},{2,1},{3,2},{4,3},{5,4},{6,5},{7,6},{8,7},{9,8},{10,9},{11,1... | collective-permute-start | bytes 294920 | tf_op jit(solution)/shard_map/ppermute | solution.py:261
  24.7 0.7 %fusion = (bf16[192]{0:T(256)(128)(2,1)S(1)}, bf16[192]{0:T(256)(128)(2,1)S(1)}, bf16[192]{0:T(256)(128)(2,1)S(1)}) fusion(f32[192]{0:T(256)} %param.12), kind=kLoop, calls=%fused_computation.4 | loop fusion | flops 1344 | bytes 1920 | tf_op jit(solution)/shard_map/convert.5
  25.4 0.1 stack.21
  25.5 0.1 stack.22
  25.6 0.1 stack.23
  25.7 0.0 copy-done.2
  25.7 0.1 copy.14
  25.8 0.2 concatenate.8
  26.0 0.0 collective-permute-done.refs_1_
  26.0 1.7 %sums.1 = f32[32,2,128]{2,1,0:T(2,128)} custom-call(f32[8,256]{1,0:T(8,128)S(1)} %get-tuple-element.9.refs_0_, bf16[6,2,16,256]{3,2,1,0:T(8,128)(2,1)S(1)} %collective-permute-done.refs_1_, bf16[6,2,16,256]{3,2,1,0:T(8,128)(2,1)S(1)} %get-tuple-element.10.refs_2_, bf16[192,440]{1,0:T(8,128)(2,1)S(1)} %bitcast.9), custom_call_target="tpu_custom_call" | custom-call | tf_op jit(solution)/shard_map/sums/pallas_call | solution.py:275
  27.7 17.6 %all-to-all-start.1 = ((f32[32,2,128]{2,1,0:T(2,128)}), f32[32,2,128]{2,1,0:T(2,128)S(1)}, u32[]{:S(2)}, u32[]{:S(2)}) async-start(f32[32,2,128]{2,1,0:T(2,128)} %sums.1), calls=%async_computation.1 | async-start | bytes 65536 | tf_op jit(solution)/shard_map/all_to_all | solution.py:288
  45.3 0.0 collective-permute-done.1.refs_3_
  45.3 0.0 copy-start
  45.3 0.0 copy-start.1
  45.3 1.4 %hidden.1 = (bf16[4,4,160,192]{3,2,1,0:T(8,128)(2,1)S(1)}, bf16[16,192,192]{2,1,0:T(8,128)(2,1)S(1)}) custom-call(f32[8,256]{1,0:T(8,128)S(1)} %get-tuple-element.9.refs_0_, bf16[6,2,16,256]{3,2,1,0:T(8,128)(2,1)S(1)} %collective-permute-done.refs_1_, bf16[6,2,16,256]{3,2,1,0:T(8,128)(2,1)S(1)} %get-tuple-element.10.refs_2_, ...), custom_call_target="tpu_custom_call" | custom-call | flops 4000000000 | bytes 2000000 | tf_op jit(solution)/shard_map/hidden/pallas_call | solution.py:289
  46.8 0.4 all-to-all-done.1.refs_1_
  47.2 0.0 copy-done
  47.2 0.0 copy-done.1
  47.2 4.2 %decode.1 = bf16[2,2,160,192]{3,2,1,0:T(8,128)(2,1)} custom-call(f32[8,256]{1,0:T(8,128)S(1)} %get-tuple-element.9.refs_0_, f32[32,2,128]{2,1,0:T(2,128)S(1)} %all-to-all-done.1.refs_1_, bf16[4,4,160,192]{3,2,1,0:T(8,128)(2,1)S(1)} %get-tuple-element.11.refs_2_, bf16[16,192,192]{2,1,0:T(8,128)(2,1)S(1)} %get-tuple-element.12.refs_3_, ...), custom_call_target="tpu_custom_call" | custom-call | tf_op jit(solution)/shard_map/decode/pallas_call | solution.py:310
  (2 shorter events, 0.0 us)
Async XLA Ops:
  0.0 25.7 %copy-start.2 = (bf16[16,27,192]{2,0,1:T(8,128)(2,1)S(1)}, bf16[16,27,192]{2,0,1:T(8,128)(2,1)}, u32[]{:S(2)}) copy-start(bf16[16,27,192]{2,0,1:T(8,128)(2,1)} %param.11) | copy-start | bytes 497668
  1.5 12.8 %all-to-all-start = ((bf16[8,2,2,2560]{3,2,1,0:T(2,128)(2,1)}), bf16[8,2,2,2560]{3,2,1,0:T(2,128)(2,1)S(1)}, u32[]{:S(2)}, u32[]{:S(2)}) async-start(bf16[8,2,2,2560]{3,2,1,0:T(2,128)(2,1)} %broadcast_in_dim.12), calls=%async_computation | async-start | bytes 327680 | tf_op jit(solution)/shard_map/all_to_all | solution.py:241
  22.1 3.9 %collective-permute-start = (bf16[6,2,16,256]{3,2,1,0:T(8,128)(2,1)S(1)}, bf16[6,2,16,256]{3,2,1,0:T(8,128)(2,1)S(1)}, u32[]{:S(2)}, u32[]{:S(2)}) collective-permute-start(bf16[6,2,16,256]{3,2,1,0:T(8,128)(2,1)S(1)} %get-tuple-element.10.refs_2_), channel_id=1, source_target_pairs={{0,1},{1,2},{2,3},{3,4},{4,5},{5,6},{6,7},{7,8},{8,9},{9,10},{10,1... | collective-permute-start | bytes 294920 | tf_op jit(solution)/shard_map/ppermute | solution.py:260
  23.4 21.9 %collective-permute-start.1 = (bf16[6,2,16,256]{3,2,1,0:T(8,128)(2,1)S(1)}, bf16[6,2,16,256]{3,2,1,0:T(8,128)(2,1)S(1)}, u32[]{:S(2)}, u32[]{:S(2)}) collective-permute-start(bf16[6,2,16,256]{3,2,1,0:T(8,128)(2,1)S(1)} %get-tuple-element.10.refs_2_), channel_id=1, source_target_pairs={{1,0},{2,1},{3,2},{4,3},{5,4},{6,5},{7,6},{8,7},{9,8},{10,9},{11,1... | collective-permute-start | bytes 294920 | tf_op jit(solution)/shard_map/ppermute | solution.py:261
  27.7 19.4 %all-to-all-start.1 = ((f32[32,2,128]{2,1,0:T(2,128)}), f32[32,2,128]{2,1,0:T(2,128)S(1)}, u32[]{:S(2)}, u32[]{:S(2)}) async-start(f32[32,2,128]{2,1,0:T(2,128)} %sums.1), calls=%async_computation.1 | async-start | bytes 65536 | tf_op jit(solution)/shard_map/all_to_all | solution.py:288
  45.3 1.9 %copy-start = (f32[192]{0:T(256)S(1)}, f32[192]{0:T(256)}, u32[]{:S(2)}) copy-start(f32[192]{0:T(256)} %param.13) | copy-start | bytes 2308
  45.3 1.9 %copy-start.1 = (f32[192]{0:T(256)S(1)}, f32[192]{0:T(256)}, u32[]{:S(2)}) copy-start(f32[192]{0:T(256)} %param.15) | copy-start | bytes 2308
